TPU v7x, 512 devices: a whole 4x8x8 slice. The times are simulated.
512 devices in a mesh: dp: 16 (over x, y_hi, core), own: 32 (over z, y_lo).
Axes of the slice: x: 4, y: 8 (y_hi: 2, y_lo: 4; y = y_hi * 4 + y_lo), z: 8, core: 2. Of those that a mesh axis runs over, the one named last changes fastest.
Arguments:
- hidden_act: bfloat16 [65536, 12288], P(('dp', 'own')), may hold values from -1000 to 1000
- out_grad: bfloat16 [65536, 4096], P(('dp', 'own')), may hold values from -1000 to 1000
- weight_grad: bfloat16 [12288, 4096], P('own', 'dp'), may hold values from -6 to 6
- owner_a: int32 [96], replicated, may hold values from 0 to 95, each once
- owner_g: int32 [32], replicated, may hold values from 0 to 31, each once
Outputs:
- a_inverse: bfloat16 [96, 128, 128], P('own')
- g_inverse: bfloat16 [32, 128, 128], P('own')
- precond: float32 [12288, 4096], P('own', 'dp')
Inputs may be any that keep to these rules, and one draw needn't show every extreme that they name: `owner_a`: slots s * 3 to s * 3 + 2 belong to index s of own; every slot holds exactly one block. `owner_g`: slots s * 1 to s + 1 - 1 belong to index s of own; every slot holds exactly one block.
All inputs are finite; a program needn't handle non-finite values. Where the computation divides by a largest or mean magnitude, that divisor is 1e-20 or more.
Results may differ from a plain program's by a relative error of at most 0.0058.
Values may be sent and summed in bfloat16 or wider, within the bound.
A program may use at most 64 MiB of HBM per device.

v0:
```python
import jax
import jax.numpy as jnp
from jax import lax
from jax.sharding import PartitionSpec as P

BLK = 128
ITERS = 14


DAMPING = 0.05


def newton(factors):
    identity = jnp.eye(factors.shape[-1], dtype=jnp.float32)
    bound_row = jnp.max(jnp.sum(jnp.abs(factors), axis=2), axis=1)
    start = identity[None, :, :] / bound_row[:, None, None]

    def refine(step_index, current):
        product = jnp.einsum("sij,sjk->sik", factors, current, precision=lax.Precision.HIGHEST)
        return jnp.einsum(
            "sij,sjk->sik", current, 2.0 * identity - product, precision=lax.Precision.HIGHEST
        )

    return lax.fori_loop(0, ITERS, refine, start)


def combine(arrived):
    return jnp.sum(arrived, axis=0)


def on_device(hidden_act, out_grad, weight_grad, owner_a, owner_g):
    owners = lax.axis_size("own")
    replicas = lax.axis_size("dp")
    own_place = lax.axis_index("own")
    dp_place = lax.axis_index("dp")
    tokens_here = hidden_act.shape[0]
    count_a = hidden_act.shape[1] // BLK
    count_g = out_grad.shape[1] // BLK
    slot_a = count_a // owners
    slot_g = count_g // owners
    token_total = tokens_here * owners * replicas
    block_of_a = (
        jnp.zeros((count_a,), jnp.int32).at[owner_a].set(jnp.arange(count_a, dtype=jnp.int32))
    )
    block_of_g = (
        jnp.zeros((count_g,), jnp.int32).at[owner_g].set(jnp.arange(count_g, dtype=jnp.int32))
    )
    act_blocks = hidden_act.reshape(tokens_here, count_a, BLK)
    grad_blocks = out_grad.reshape(tokens_here, count_g, BLK)
    terms_a = jnp.einsum("tbi,tbj->bij", act_blocks, act_blocks, preferred_element_type=jnp.float32)
    terms_g = jnp.einsum(
        "tbi,tbj->bij", grad_blocks, grad_blocks, preferred_element_type=jnp.float32
    )
    send_a = jnp.take(terms_a, block_of_a, axis=0).reshape(owners, slot_a, BLK, BLK)
    send_g = jnp.take(terms_g, block_of_g, axis=0).reshape(owners, slot_g, BLK, BLK)
    outgoing = jnp.concatenate((send_a, send_g), axis=1)
    summed = combine(lax.all_to_all(outgoing, "own", split_axis=0, concat_axis=0, tiled=True))
    summed = lax.psum(summed, "dp")
    identity = jnp.eye(BLK, dtype=jnp.float32)
    factors = summed / token_total + DAMPING * identity
    panels = newton(factors).astype(jnp.bfloat16)
    a_panels = panels[:slot_a]
    g_panels = panels[slot_a:]
    every_a, every_g = (
        lax.all_gather(a_panels, "own", axis=0, tiled=True),
        lax.all_gather(g_panels, "own", axis=0, tiled=True),
    )
    row_blocks = weight_grad.shape[0] // BLK
    col_blocks = weight_grad.shape[1] // BLK
    want_a = lax.dynamic_slice_in_dim(owner_a, own_place * row_blocks, row_blocks)
    want_g = lax.dynamic_slice_in_dim(owner_g, dp_place * col_blocks, col_blocks)
    pick_a = jnp.take(every_a, want_a, axis=0)
    pick_g = jnp.take(every_g, want_g, axis=0)
    grad_rows = weight_grad.reshape(row_blocks, BLK, weight_grad.shape[1])
    left_side = jnp.einsum(
        "bij,bjc->bic", pick_a, grad_rows, preferred_element_type=jnp.float32
    ).astype(jnp.bfloat16)
    left_side = left_side.reshape(row_blocks * BLK, col_blocks, BLK)
    precond = jnp.einsum("rcj,cjk->rck", left_side, pick_g, preferred_element_type=jnp.float32)
    return (a_panels, g_panels, precond.reshape(row_blocks * BLK, col_blocks * BLK))


def solution(mesh):
    placed = (P(("dp", "own"), None), P(("dp", "own"), None), P("own", "dp"), P(), P())
    return jax.shard_map(
        on_device,
        mesh=mesh,
        in_specs=placed,
        out_specs=(P("own", None, None), P("own", None, None), P("own", "dp")),
        check_vma=False,
    )
```

profile of v0, /device:TPU:6, one launch (start us, length us, event | category | flops | bytes accessed | tf_op | source)
XLA Modules:
  0.0 793.9 jit_solution(4032415463555060179)
XLA Ops:
  10.3 3.9 fusion.3
  14.3 3.4 fusion.7
  17.7 6.4 gather_fusion
  24.1 5.9 broadcast_select_fusion
  30.0 3.6 gather_fusion.1
  33.7 1.8 fusion.6
  35.5 3.6 pad_maximum_fusion
  39.1 199.9 %all_to_all.5 = f32[32,4,128,128]{3,2,1,0:T(8,128)} all-to-all(f32[32,4,128,128]{3,2,1,0:T(8,128)S(1)} %pad_maximum_fusion), channel_id=1, replica_groups=mesh['dp'=16,'own'=32] {'own'}, dimensions={0} | all-to-all | bytes 16777216 | tf_op jit(solution)/shard_map/all_to_all | solution.py:57
  239.0 4.5 reduce_sum.18
  243.7 172.3 %all-reduce.2.cloned.1.call-done = f32[4,128,128]{2,1,0:T(8,128)} async-done(((f32[4,128,128]{2,1,0:T(8,128)}), f32[4,128,128]{2,1,0:T(8,128)}) %all-reduce.2.cloned.1.call-update) | async-done | bytes 262160 | tf_op jit(solution)/shard_map/psum | solution.py:58
  416.0 1.7 abs_reduce_fusion
  417.9 32.0 %while.11 = (s32[]{:T(128)}, f32[4,128,128]{1,2,0:T(8,128)S(1)}, f32[4,128,128]{2,1,0:T(8,128)}, s32[]{:T(128)}) while((s32[]{:T(128)}, f32[4,128,128]{1,2,0:T(8,128)S(1)}, f32[4,128,128]{2,1,0:T(8,128)}, s32[]{:T(128)}) %tuple.32), condition=%wide.region_7.8_spmd.clone, body=%wide.region_6.7_spmd.clone.sunk | while | flops 201424896 | bytes 2228277 | solution.py:24
  418.0 1.6 convolution_subtract_fusion.2
  422.6 1.6 convolution_subtract_fusion.2
  424.8 1.6 convolution_subtract_fusion.2
  429.4 1.6 convolution_subtract_fusion.2
  431.7 1.6 convolution_subtract_fusion.2
  436.3 1.6 convolution_subtract_fusion.2
  438.6 1.6 convolution_subtract_fusion.2
  445.4 1.6 convolution_subtract_fusion.2
  451.7 161.9 %all-gather.3.cloned.1.call-done = bf16[32,128,128]{2,1,0:T(8,128)(2,1)} async-done(((bf16[1,128,128]{2,1,0:T(8,128)(2,1)}), bf16[32,128,128]{2,1,0:T(8,128)(2,1)}) %all-gather.3.cloned.1.call-update) | async-done | bytes 1048592 | tf_op jit(solution)/shard_map/all_gather | solution.py:66
  613.6 2.4 gather_fusion.2
  616.0 164.7 %all-gather.5.cloned.1.call-done = bf16[96,128,128]{2,1,0:T(8,128)(2,1)} async-done(((bf16[3,128,128]{2,1,0:T(8,128)(2,1)}), bf16[96,128,128]{2,1,0:T(8,128)(2,1)}) %all-gather.5.cloned.1.call-update) | async-done | bytes 3145744 | tf_op jit(solution)/shard_map/all_gather | solution.py:65
  780.7 2.5 gather_fusion.3
  (89 shorter events, 27.8 us)
Async XLA Ops:
  7.2 3.2 copy-start
  7.2 408.8 %all-reduce.2.cloned.1.call-start = ((), (), s32[]{:S(2)}) async-start(), calls=%async_computation.1 | async-start | bytes 524288 | tf_op jit(solution)/shard_map/psum | solution.py:58
  243.5 370.1 %all-gather.3.cloned.1.call-start = ((), (), s32[]{:S(2)}) async-start(), calls=%async_computation.2 | async-start | bytes 1081344 | tf_op jit(solution)/shard_map/all_gather | solution.py:66
  417.9 33.6 %copy-start.1 = (s32[96]{0:T(128)S(1)}, s32[96]{0:T(128)}, u32[]{:S(2)}) copy-start(s32[96]{0:T(128)} %param.10) | copy-start | bytes 1156
  417.9 33.7 %copy-start.2 = (s32[32]{0:T(128)S(1)}, s32[32]{0:T(128)}, u32[]{:S(2)}) copy-start(s32[32]{0:T(128)} %param.11) | copy-start | bytes 388
  450.7 330.0 %all-gather.5.cloned.1.call-start = ((), (), s32[]{:S(2)}) async-start(), calls=%async_computation.3 | async-start | bytes 3244032 | tf_op jit(solution)/shard_map/all_gather | solution.py:65
Sparse Core Ops, SparseCore 0:
  243.7 172.2 all-reduce.1
  450.9 162.7 all-gather.2
  616.5 164.2 all-gather.4
where the time goes:
time: 795 us; the launch traced here: 794 us
  waiting for transfers between devices  499 us (63%)
  blocking collectives  200 us (25%)
  matrix products  40.7 us (5%)
  local copies, waits for them, and re-layouts  19.9 us (3%)
  other arithmetic  19.6 us (2%)
  between operations  13.9 us (2%)
    all_to_all x1, blocking collectives, on_device(): lax.all_to_all(outgoing, 'own', split_axis=0, concat_axis=0, tiled=True)  200 us
    psum x1, waiting for transfers between devices, on_device(): summed = lax.psum(summed, 'dp')  172 us
    all_gather x1, waiting for transfers between devices, on_device(): lax.all_gather(a_panels, 'own', axis=0, tiled=True)  165 us
    all_gather x1, waiting for transfers between devices, on_device(): lax.all_gather(g_panels, 'own', axis=0, tiled=True)  162 us
    dot_general x14, matrix products, refine(): jnp.einsum('sij,sjk->sik', factors, current, precision=lax.Precision.HIGH...  22.6 us
  transfers between devices with their start and end apart: 3, of which 3 were waited for; matrix products, arithmetic and copies ran while one was open for 0% of the time, Pallas kernels for 0%

commit v1 on v0

v1 whole, which is shorter than its diff:
```python
import jax
import jax.numpy as jnp
from jax import lax
from jax.experimental import pallas as pl
from jax.experimental.pallas import tpu as pltpu
from jax.sharding import PartitionSpec as P

BLK = 128
ITERS = 14
DAMPING = 0.05
NX, NY, NZ, NYL = 4, 8, 8, 4
MESH = pl.DeviceIdType.MESH
F32 = jnp.float32
BF16 = jnp.bfloat16


def place():
    dp = lax.axis_index("dp")
    own = lax.axis_index("own")
    return dp // 4, ((dp // 2) % 2) * NYL + own % NYL, own // NYL, dp % 2


def device(x, y, z, c):
    return (x * 4 + (y // NYL) * 2 + c, z * NYL + y % NYL)


def send(src, dst, send_sem, recv_sem, to):
    copy = pltpu.make_async_remote_copy(
        src_ref=src, dst_ref=dst, send_sem=send_sem, recv_sem=recv_sem,
        device_id=to, device_id_type=MESH,
    )
    copy.start()


def arrived(ref, sem):
    pltpu.make_async_copy(ref, ref, sem).wait()


def gram_kernel(hid, grd, m_out, d_out,
                raw, ta, tb, tg, ra, rb, rg, a2, b2, g2, ra2, rb2, rg2, a3, x3, ra3, rx3, fin,
                s_loc, s_raw_s, s_raw_r, s_a, r_a, s_b, r_b, s_g, r_g,
                s_a2, r_a2, s_b2, r_b2, s_g2, r_g2, s_a3, r_a3, s_x3, r_x3, s_f, r_f):
    x, y, z, c = place()
    sib = device(x, y, z, 1 - c)

    barrier = pltpu.get_barrier_semaphore()
    pl.semaphore_signal(barrier, inc=1, device_id=sib, device_id_type=MESH)
    for j in range(1, NX):
        pl.semaphore_signal(barrier, inc=1, device_id=device((x + j) % NX, y, z, c), device_id_type=MESH)
    for j in range(1, NY):
        pl.semaphore_signal(barrier, inc=1, device_id=device(x, (y + j) % NY, z, c), device_id_type=MESH)
    for j in range(1, NZ):
        pl.semaphore_signal(barrier, inc=1, device_id=device(x, y, (z + j) % NZ, c), device_id_type=MESH)

    def local_parts(zz, core, rows):
        return (
            (hid.at[:, pl.ds(pl.multiple_of(6144 * core + 768 * zz, 128), 768)],
             raw.at[rows, pl.ds(pl.multiple_of(1024 * zz, 128), 768)]),
            (grd.at[:, pl.ds(pl.multiple_of(2048 * core + 256 * zz, 128), 256)],
             raw.at[rows, pl.ds(pl.multiple_of(1024 * zz + 768, 128), 256)]),
        )

    low, high = pl.ds(0, 128), pl.ds(128, 128)

    @pl.loop(0, NZ)
    def _(i):
        zz = (z + 1 + i) % NZ
        for k, (src, dst) in enumerate(local_parts(zz, c, low)):
            pltpu.make_async_copy(src, dst, s_loc.at[i, k]).start()

    pl.semaphore_wait(barrier, 1 + (NX - 1) + (NY - 1) + (NZ - 1))

    @pl.loop(0, NZ)
    def _(i):
        zz = (z + 1 + i) % NZ
        for k, (src, dst) in enumerate(local_parts(zz, 1 - c, high)):
            send(src, dst, s_raw_s.at[i, k], s_raw_r.at[i, k], sib)

    row8 = lax.broadcasted_iota(jnp.int32, (BLK, BLK), 0) // 8
    col8 = lax.broadcasted_iota(jnp.int32, (BLK, BLK), 1) // 8
    upper = row8 <= col8
    middle = row8 == col8

    def gram(zz, k):
        cols = pl.ds(pl.multiple_of(1024 * zz + BLK * k, BLK), BLK)
        tok = raw[:, cols]
        return lax.dot_general(tok, tok, (((0,), (0,)), ((), ())), preferred_element_type=F32)

    @pl.loop(0, NZ)
    def _(i):
        zz = (z + 1 + i) % NZ
        for k, (src, dst) in enumerate(local_parts(zz, c, low)):
            pltpu.make_async_copy(src, dst, s_loc.at[i, k]).wait()
        for k, (src, dst) in enumerate(local_parts(zz, c, high)):
            arrived(dst, s_raw_r.at[i, k])
        for xx in range(NX):
            first = gram(zz, 2 * xx)
            second = gram(zz, 2 * xx + 1)
            packed = jnp.where(upper, first, second).reshape(NY, 2, 8, BLK)
            extra = jnp.sum(jnp.where(middle, second, 0.0).reshape(16, 8, BLK), axis=0)
            ta[zz, xx, pl.ds(0, NY)] = packed[:, 0]
            ta[zz, xx, NY] = extra
            if xx < 2:
                tb[:, i, xx] = packed[:, 1]
            else:
                tg[zz, xx - 2] = packed[:, 1]
        for j in range(1, NX):
            to = (x + j) % NX
            send(ta.at[zz, to], ra.at[j - 1, zz], s_a.at[j - 1, i], r_a.at[j - 1, i], device(to, y, z, c))

        @pl.when(i < NZ - 1)
        def _():
            send(tg.at[zz], rg.at[i], s_g.at[i], r_g.at[i], device(x, y, zz, c))

        @pl.when(i % 4 == 3)
        def _():
            half = i // 4
            for j in range(1, NY):
                to = (y + j) % NY
                send(tb.at[to, pl.ds(4 * half, 4)], rb.at[j - 1, pl.ds(4 * half, 4)],
                     s_b.at[j - 1, half], r_b.at[j - 1, half], device(x, to, z, c))

    @pl.loop(0, NZ)
    def _(i):
        zz = (z + 1 + i) % NZ
        total = ta[zz, x]
        for j in range(NX - 1):
            arrived(ra.at[j, zz], r_a.at[j, i])
            total = total + ra[j, zz]
        a2[zz] = total

        @pl.when(i < NZ - 1)
        def _():
            send(a2.at[zz], ra2.at[i], s_a2.at[i], r_a2.at[i], device(x, y, zz, c))

    for j in range(NZ - 1):
        arrived(rg.at[j], r_g.at[j])
    for k in range(2):
        total = tg[z, k]
        for j in range(NZ - 1):
            total = total + rg[j, k]
        for yy in range(NY):
            g2[yy, k] = total[yy]
    for j in range(1, NY):
        to = (y + j) % NY
        send(g2.at[to], rg2.at[j - 1], s_g2.at[j - 1], r_g2.at[j - 1], device(x, to, z, c))

    for j in range(NY - 1):
        for half in range(2):
            arrived(rb.at[j, pl.ds(4 * half, 4)], r_b.at[j, half])

    @pl.loop(0, NZ)
    def _(i):
        total = tb[y, i]
        for j in range(NY - 1):
            total = total + rb[j, i]
        b2[i] = total
        zz = (z + 1 + i) % NZ

        @pl.when(i < NZ - 1)
        def _():
            send(b2.at[i], rb2.at[i], s_b2.at[i], r_b2.at[i], device(x, y, zz, c))

    total = a2[z]
    for j in range(NZ - 1):
        arrived(ra2.at[j], r_a2.at[j])
        total = total + ra2[j]
    for yy in range(NY):
        a3[yy, 0] = total[yy]
        a3[yy, 1] = total[NY]
    for j in range(1, NY):
        to = (y + j) % NY
        send(a3.at[to], ra3.at[j - 1], s_a3.at[j - 1], r_a3.at[j - 1], device(x, to, z, c))

    total = g2[y]
    for j in range(NY - 1):
        arrived(rg2.at[j], r_g2.at[j])
        total = total + rg2[j]
    x3[2] = total[0]
    x3[3] = total[1]
    total = b2[NZ - 1]
    for j in range(NZ - 1):
        arrived(rb2.at[j], r_b2.at[j])
        total = total + rb2[j]
    x3[0] = total[0]
    x3[1] = total[1]
    for j in range(1, NX):
        to = (x + j) % NX
        send(x3.at[to], rx3.at[j - 1], s_x3.at[j - 1], r_x3.at[j - 1], device(to, y, z, c))

    total = a3[y]
    for j in range(NY - 1):
        arrived(ra3.at[j], r_a3.at[j])
        total = total + ra3[j]
    fin[0] = total[0]
    d_out[...] = total[1]
    total = x3[x]
    for j in range(NX - 1):
        arrived(rx3.at[j], r_x3.at[j])
        total = total + rx3[j]
    fin[1] = total

    m_out[y] = fin[...]
    for j in range(1, NY):
        to = (y + j) % NY
        send(fin, m_out.at[y], s_f.at[j - 1], r_f.at[j - 1], device(x, to, z, c))
    for j in range(1, NY):
        arrived(m_out.at[(y - j + NY) % NY], r_f.at[j - 1])

    @pl.loop(0, NZ)
    def _(i):
        zz = (z + 1 + i) % NZ
        for k, (src, dst) in enumerate(local_parts(zz, 1 - c, high)):
            arrived(src, s_raw_s.at[i, k])
        for j in range(NX - 1):
            arrived(ta.at[zz, x], s_a.at[j, i])

    for j in range(NZ - 1):
        arrived(tg.at[j], s_g.at[j])
        arrived(a2.at[j], s_a2.at[j])
        arrived(b2.at[j], s_b2.at[j])
    for j in range(NY - 1):
        for half in range(2):
            arrived(tb.at[j, pl.ds(4 * half, 4)], s_b.at[j, half])
        arrived(g2.at[j], s_g2.at[j])
        arrived(a3.at[j], s_a3.at[j])
        arrived(fin, s_f.at[j])
    for j in range(NX - 1):
        arrived(x3.at[j], s_x3.at[j])


def gram_sums(hid, grd):
    dma = pltpu.SemaphoreType.DMA
    tile = (8, BLK)
    vm = pltpu.VMEM
    return pl.pallas_call(
        gram_kernel,
        out_shape=(jax.ShapeDtypeStruct((NY, 2) + tile, F32), jax.ShapeDtypeStruct(tile, F32)),
        in_specs=[pl.BlockSpec(memory_space=pl.ANY)] * 2,
        out_specs=[pl.BlockSpec(memory_space=pltpu.VMEM)] * 2,
        scratch_shapes=[
            vm((256, 8192), BF16),
            vm((NZ, NX, NY + 1) + tile, F32),
            vm((NY, NZ, 2) + tile, F32),
            vm((NZ, 2, NY) + tile, F32),
            vm((NX - 1, NZ, NY + 1) + tile, F32),
            vm((NY - 1, NZ, 2) + tile, F32),
            vm((NZ - 1, 2, NY) + tile, F32),
            vm((NZ, NY + 1) + tile, F32),
            vm((NZ, 2) + tile, F32),
            vm((NY, 2) + tile, F32),
            vm((NZ - 1, NY + 1) + tile, F32),
            vm((NZ - 1, 2) + tile, F32),
            vm((NY - 1, 2) + tile, F32),
            vm((NY, 2) + tile, F32),
            vm((NX,) + tile, F32),
            vm((NY - 1, 2) + tile, F32),
            vm((NX - 1,) + tile, F32),
            vm((2,) + tile, F32),
            dma((NZ, 2)), dma((NZ, 2)), dma((NZ, 2)),
            dma((NX - 1, NZ)), dma((NX - 1, NZ)),
            dma((NY - 1, 2)), dma((NY - 1, 2)),
            dma((NZ - 1,)), dma((NZ - 1,)),
            dma((NZ - 1,)), dma((NZ - 1,)),
            dma((NZ - 1,)), dma((NZ - 1,)),
            dma((NY - 1,)), dma((NY - 1,)),
            dma((NY - 1,)), dma((NY - 1,)),
            dma((NX - 1,)), dma((NX - 1,)),
            dma((NY - 1,)), dma((NY - 1,)),
        ],
        compiler_params=pltpu.CompilerParams(
            collective_id=0, has_side_effects=True, vmem_limit_bytes=40 * 2**20
        ),
        cost_estimate=pl.CostEstimate(flops=2 * 64 * 256 * BLK * BLK, bytes_accessed=4 * 2**20, transcendentals=0),
        name="gram_sums",
    )(hid, grd)


def split3(value):
    high = value.astype(BF16)
    rest = value - high.astype(F32)
    mid = rest.astype(BF16)
    return high, mid, (rest - mid.astype(F32)).astype(BF16)


def product(left, right):
    lh, lm, ll = split3(left)
    rh, rm, rl = split3(right)

    def dot(a, b):
        return jnp.dot(a, b, preferred_element_type=F32)

    small = dot(jnp.concatenate((lm, ll), axis=1), jnp.concatenate((rm, rh), axis=0))
    middle = dot(jnp.concatenate((lh, lm), axis=1), jnp.concatenate((rm, rh), axis=0))
    large = dot(jnp.concatenate((lh, lh), axis=1), jnp.concatenate((rh, rl), axis=0))
    return large + (middle + small)


def newton_kernel(token_total, m_ref, d_ref, x_ref):
    _, y, _, _ = place()
    second = (y // NYL) == 1
    packed = m_ref[...].reshape(BLK, BLK)
    extra = jnp.broadcast_to(d_ref[...][None], (16, 8, BLK)).reshape(BLK, BLK)
    row = lax.broadcasted_iota(jnp.int32, (BLK, BLK), 0)
    col = lax.broadcasted_iota(jnp.int32, (BLK, BLK), 1)
    turned = packed.T
    first_block = jnp.where(row // 8 <= col // 8, packed, turned)
    second_block = jnp.where(row // 8 == col // 8, extra, jnp.where(row // 8 > col // 8, packed, turned))
    sums = jnp.where(second, second_block, first_block)
    identity = jnp.where(row == col, 1.0, 0.0)
    factor = sums / token_total + DAMPING * identity
    bound = jnp.max(jnp.sum(jnp.abs(factor), axis=1, keepdims=True), axis=0, keepdims=True)
    both = jnp.concatenate((factor / bound, identity / bound), axis=1)

    def refine(step, both):
        return 2.0 * both - product(both[:, :BLK], both)

    both = lax.fori_loop(0, ITERS, refine, both)
    x_ref[...] = both[:, BLK:].astype(BF16)


def newton(token_total, packed, extra):
    return pl.pallas_call(
        lambda *refs: newton_kernel(token_total, *refs),
        out_shape=jax.ShapeDtypeStruct((BLK, BLK), BF16),
        in_specs=[pl.BlockSpec(memory_space=pltpu.VMEM)] * 2,
        out_specs=pl.BlockSpec(memory_space=pltpu.VMEM),
        cost_estimate=pl.CostEstimate(flops=2 * 14 * 6 * 2 * BLK**3, bytes_accessed=2**17, transcendentals=0),
        name="newton",
    )(packed, extra)


def spread_kernel(inv, owner_a, owner_g, r4, r5,
                  p0, kept, s4, s_0, r_0, s_z, r_z, s_k, r_k, s_4, r_4, s_5, r_5):
    x, y, z, c = place()
    yh, yl = y // NYL, y % NYL
    dp, own = lax.axis_index("dp"), lax.axis_index("own")
    e = 2 * x + yh
    sib = device(x, y, z, 1 - c)

    def peer(j):
        other = (e + j) % 8
        return other, device(other // 2, (other % 2) * NYL + yl, z, c)

    barrier = pltpu.get_barrier_semaphore()
    pl.semaphore_signal(barrier, inc=1, device_id=sib, device_id_type=MESH)
    for j in range(1, 8):
        pl.semaphore_signal(barrier, inc=1, device_id=peer(j)[1], device_id_type=MESH)
    for j in range(1, NZ):
        pl.semaphore_signal(barrier, inc=1, device_id=device(x, y, (z + j) % NZ, c), device_id_type=MESH)

    def find_a(b, found):
        at = owner_a[b] - 3 * own
        return tuple(jnp.where(at == k, b, found[k]) for k in range(3))

    def find_g(b, found):
        return jnp.where(owner_g[b] == own, b, found)

    zero = jnp.int32(0)
    slot_a = lax.fori_loop(0, 96, find_a, (zero, zero, zero))
    slot_g = lax.fori_loop(0, 32, find_g, zero)

    def at_a(b):
        return b // 48, (b % 48) // 6, b % 6

    def at_g(b):
        return b // 16, (b % 16) // 2, 6 + b % 2

    want = [tuple(jnp.where(c == 0, s, n) for s, n in zip(at_a(slot_a[k]), at_a(3 * own + k))) for k in range(3)]
    want.append(at_g(slot_g))

    pl.semaphore_wait(barrier, 1 + 7 + (NZ - 1))

    for j in range(1, 8):
        other, to = peer(j)
        send(inv.at[pl.ds(pl.multiple_of(16 * other, 16), 16)], p0.at[e], s_0.at[j - 1], r_0.at[j - 1], to)
    p0[e] = inv[pl.ds(pl.multiple_of(16 * e, 16), 16), :]
    for j in range(1, 8):
        arrived(p0.at[(e - j + 8) % 8], r_0.at[j - 1])
    for j in range(1, NZ):
        send(p0, kept.at[c, z], s_z.at[j - 1], r_z.at[j - 1], device(x, y, (z + j) % NZ, c))
    send(p0, kept.at[c, z], s_k.at[0], r_k.at[0], sib)
    kept[c, z] = p0[...]
    for j in range(1, NZ):
        zz = (z - j + NZ) % NZ
        arrived(kept.at[c, zz], r_z.at[j - 1])
        send(kept.at[c, zz], kept.at[c, zz], s_k.at[j], r_k.at[j], sib)
    for j in range(NZ):
        arrived(kept.at[1 - c, (z - j + NZ) % NZ], r_k.at[j])

    shared = [kept[w] for w in want]
    for j in range(1, 9):
        other, to = peer(j)
        for k in range(4):
            s4[other, k] = shared[k]
        for k in range(2):
            s4[other, 4 + k] = kept[at_g(2 * (2 * other + c) + k)]
        if j < 8:
            send(s4.at[other], r4.at[e], s_4.at[j - 1], r_4.at[j - 1], to)
    r4[e] = s4[e]
    send(s4.at[e, pl.ds(0, 4)], r5.at[e], s_5.at[0], r_5.at[0], sib)
    for j in range(1, 8):
        other = (e - j + 8) % 8
        arrived(r4.at[other], r_4.at[j - 1])
        send(r4.at[other, pl.ds(0, 4)], r5.at[other], s_5.at[j], r_5.at[j], sib)
    for j in range(8):
        arrived(r5.at[(e - j + 8) % 8], r_5.at[j])

    for j in range(7):
        arrived(p0.at[0], s_0.at[j])
        arrived(p0, s_z.at[j])
        arrived(s4.at[0], s_4.at[j])
    for j in range(8):
        arrived(p0, s_k.at[j])
        arrived(r5.at[0], s_5.at[j])


def spread(inv, owner_a, owner_g):
    dma = pltpu.SemaphoreType.DMA
    vm = pltpu.VMEM
    piece = (16, BLK)
    return pl.pallas_call(
        spread_kernel,
        out_shape=(jax.ShapeDtypeStruct((8, 6) + piece, BF16), jax.ShapeDtypeStruct((8, 4) + piece, BF16)),
        in_specs=[pl.BlockSpec(memory_space=pltpu.VMEM)] + [pl.BlockSpec(memory_space=pltpu.SMEM)] * 2,
        out_specs=[pl.BlockSpec(memory_space=pltpu.VMEM)] * 2,
        scratch_shapes=[
            vm((8,) + piece, BF16), vm((2, NZ, 8) + piece, BF16), vm((8, 6) + piece, BF16),
            dma((7,)), dma((7,)), dma((7,)), dma((7,)), dma((8,)), dma((8,)),
            dma((7,)), dma((7,)), dma((8,)), dma((8,)),
        ],
        compiler_params=pltpu.CompilerParams(
            collective_id=1, has_side_effects=True, vmem_limit_bytes=16 * 2**20
        ),
        name="spread_inverses",
    )(inv, owner_a, owner_g)


def apply_kernel(r4, r5, w, a_out, g_out, p_out):
    _, _, _, c = place()

    def whole(ref, k):
        return ref[:, k].reshape(BLK, BLK)

    mine = [whole(r4, k) for k in range(6)]
    theirs = [whole(r5, k) for k in range(4)]
    even = c == 0
    for k in range(3):
        a_out[k] = jnp.where(even, mine[k], theirs[k])
    g_out[0] = mine[3]
    for k in range(3):
        nat = jnp.where(even, theirs[k], mine[k])
        rows = pl.ds(BLK * k, BLK)
        left = jnp.dot(nat, w[rows, :], preferred_element_type=F32).astype(BF16)
        for m in range(2):
            cols = slice(BLK * m, BLK * (m + 1))
            p_out[rows, cols] = jnp.dot(left[:, cols], mine[4 + m], preferred_element_type=F32)


def apply_inverses(r4, r5, w):
    return pl.pallas_call(
        apply_kernel,
        out_shape=(
            jax.ShapeDtypeStruct((3, BLK, BLK), BF16),
            jax.ShapeDtypeStruct((1, BLK, BLK), BF16),
            jax.ShapeDtypeStruct(w.shape, F32),
        ),
        name="apply_inverses",
    )(r4, r5, w)


def on_device(hidden_act, out_grad, weight_grad, owner_a, owner_g):
    token_total = hidden_act.shape[0] * lax.axis_size("own") * lax.axis_size("dp")
    packed, extra = gram_sums(hidden_act, out_grad)
    inverse = newton(token_total, packed, extra)
    r4, r5 = spread(inverse, owner_a, owner_g)
    return apply_inverses(r4, r5, weight_grad)


def solution(mesh):
    placed = (P(("dp", "own"), None), P(("dp", "own"), None), P("own", "dp"), P(), P())
    return jax.shard_map(
        on_device,
        mesh=mesh,
        in_specs=placed,
        out_specs=(P("own", None, None), P("own", None, None), P("own", "dp")),
        check_vma=False,
    )
```

time: 795 us -> 92.2 us (0.12)
  the two profiles are of different devices: /device:TPU:6 before, /device:TPU:1 now
where the time goes in v1:
time: 92.2 us; the launch traced here: 91.9 us
  Pallas kernels  84.8 us (92%)
  local copies, waits for them, and re-layouts  6.4 us (7%)
    pallas_call x1, Pallas kernels, gram_sums(): pl.pallas_call(gram_kernel, out_shape=(jax.ShapeDtypeStruct((NY, 2) + til...  49.9 us
    pallas_call x1, Pallas kernels, spread(): pl.pallas_call(spread_kernel, out_shape=(jax.ShapeDtypeStruct((8, 6) + pi...  27.9 us
    unnamed x18, local copies, waits for them, and re-layouts  6.4 us
    pallas_call x1, Pallas kernels, newton(): pl.pallas_call(lambda *refs: newton_kernel(token_total, *refs), out_shape...  4.75 us
    pallas_call x1, Pallas kernels, apply_inverses(): pl.pallas_call(apply_kernel, out_shape=(jax.ShapeDtypeStruct((3, BLK, BLK...  2.2 us

profile of v1, /device:TPU:1, one launch (start us, length us, event | category | flops | bytes accessed | tf_op | source)
XLA Modules:
  0.0 91.9 jit_solution(239848083126825458)
XLA Ops:
  0.6 0.0 copy-start
  0.6 1.9 %copy-done = bf16[128,12288]{1,0:T(8,128)(2,1)S(1)} copy-done((bf16[128,12288]{1,0:T(8,128)(2,1)S(1)}, bf16[128,12288]{1,0:T(8,128)(2,1)}, u32[]{:S(2)}) %copy-start) | copy-done | bytes 3145752
  2.5 0.0 copy-start.1
  2.5 1.2 %copy-done.1 = bf16[128,4096]{1,0:T(8,128)(2,1)S(1)} copy-done((bf16[128,4096]{1,0:T(8,128)(2,1)S(1)}, bf16[128,4096]{1,0:T(8,128)(2,1)}, u32[]{:S(2)}) %copy-start.1) | copy-done | bytes 1048600
  3.7 0.0 copy-start.5
  3.7 0.0 copy-start.6
  3.8 49.9 %gram_sums.1 = (f32[8,2,8,128]{3,2,1,0:T(8,128)S(1)}, f32[8,128]{1,0:T(8,128)S(1)}) custom-call(bf16[128,12288]{1,0:T(8,128)(2,1)S(1)} %copy-done, bf16[128,4096]{1,0:T(8,128)(2,1)S(1)} %copy-done.1), custom_call_target="tpu_custom_call" | custom-call | flops 536870912 | bytes 4194304 | tf_op jit(solution)/shard_map/gram_sums/pallas_call | solution.py:236
  53.6 0.0 copy-start.7
  53.6 0.6 copy-done.7
  54.3 0.0 copy-start.8
  54.3 0.6 copy-done.8
  54.9 4.7 %newton.1.inv = bf16[128,128]{1,0:T(8,128)(2,1)} custom-call(f32[8,2,8,128]{3,2,1,0:T(8,128)} %copy-done.7, f32[8,128]{1,0:T(8,128)} %copy-done.8), custom_call_target="tpu_custom_call" | custom-call | flops 704643072 | bytes 131072 | tf_op jit(solution)/shard_map/newton/pallas_call | solution.py:323
  59.6 0.0 copy-done.5
  59.6 0.0 copy-done.6
  59.6 0.0 copy-start.4
  59.6 0.8 copy-done.4
  60.4 27.9 %spread_inverses.1 = (bf16[8,6,16,128]{3,2,1,0:T(8,128)(2,1)S(1)}, bf16[8,4,16,128]{3,2,1,0:T(8,128)(2,1)S(1)}) custom-call(bf16[128,128]{1,0:T(8,128)(2,1)S(1)} %copy-done.4, s32[96]{0:T(128)S(1)} %copy-done.5, s32[32]{0:T(128)S(1)} %copy-done.6), custom_call_target="tpu_custom_call" | custom-call | tf_op jit(solution)/shard_map/spread_inverses/pallas_call | solution.py:422
  88.3 0.0 copy-start.2
  88.3 0.7 copy-done.2
  89.0 0.0 copy-start.3
  89.0 0.6 copy-done.3
  89.7 2.2 %apply_inverses.1 = (bf16[3,128,128]{2,1,0:T(8,128)(2,1)}, bf16[1,128,128]{2,1,0:T(8,128)(2,1)}, f32[384,256]{1,0:T(8,128)}) custom-call(bf16[8,6,16,128]{3,2,1,0:T(8,128)(2,1)} %copy-done.2, bf16[8,4,16,128]{3,2,1,0:T(8,128)(2,1)} %copy-done.3, bf16[384,256]{1,0:T(8,128)(2,1)} %w.1), custom_call_target="tpu_custom_call" | custom-call | tf_op jit(solution)/shard_map/apply_inverses/pallas_call | solution.py:461
Async XLA Ops:
  0.6 1.9 %copy-start = (bf16[128,12288]{1,0:T(8,128)(2,1)S(1)}, bf16[128,12288]{1,0:T(8,128)(2,1)}, u32[]{:S(2)}) copy-start(bf16[128,12288]{1,0:T(8,128)(2,1)} %hid.1) | copy-start | bytes 9437188
  2.5 1.2 %copy-start.1 = (bf16[128,4096]{1,0:T(8,128)(2,1)S(1)}, bf16[128,4096]{1,0:T(8,128)(2,1)}, u32[]{:S(2)}) copy-start(bf16[128,4096]{1,0:T(8,128)(2,1)} %grd.1) | copy-start | bytes 3145732
  3.7 55.9 %copy-start.5 = (s32[96]{0:T(128)S(1)}, s32[96]{0:T(128)}, u32[]{:S(2)}) copy-start(s32[96]{0:T(128)} %owner_a.1) | copy-start | bytes 1156
  3.7 55.9 %copy-start.6 = (s32[32]{0:T(128)S(1)}, s32[32]{0:T(128)}, u32[]{:S(2)}) copy-start(s32[32]{0:T(128)} %owner_g.1) | copy-start | bytes 388
  53.6 0.6 copy-start.7
  54.3 0.6 copy-start.8
  59.6 0.8 copy-start.4
  88.3 0.7 copy-start.2
  89.0 0.6 copy-start.3

commit v2 on v1

--- a/solution.py
+++ b/solution.py
@@ -269,7 +269,7 @@
             dma((NY - 1,)), dma((NY - 1,)),
         ],
         compiler_params=pltpu.CompilerParams(
-            collective_id=0, has_side_effects=True, vmem_limit_bytes=40 * 2**20
+            collective_id=0, has_side_effects=True, vmem_limit_bytes=62 * 2**20
         ),
         cost_estimate=pl.CostEstimate(flops=2 * 64 * 256 * BLK * BLK, bytes_accessed=4 * 2**20, transcendentals=0),
         name="gram_sums",
@@ -296,9 +296,14 @@
     return large + (middle + small)
 
 
-def newton_kernel(token_total, m_ref, d_ref, x_ref):
+def newton_kernel(token_total, m_hbm, d_hbm, x_hbm, m_ref, d_ref, x_ref, sem):
+    loads = [pltpu.make_async_copy(m_hbm, m_ref, sem.at[0]), pltpu.make_async_copy(d_hbm, d_ref, sem.at[1])]
+    for load in loads:
+        load.start()
+    for load in loads:
+        load.wait()
     _, y, _, _ = place()
-    second = (y // NYL) == 1
+    second = (y % 2) == 1
     packed = m_ref[...].reshape(BLK, BLK)
     extra = jnp.broadcast_to(d_ref[...][None], (16, 8, BLK)).reshape(BLK, BLK)
     row = lax.broadcasted_iota(jnp.int32, (BLK, BLK), 0)
@@ -317,37 +322,42 @@
 
     both = lax.fori_loop(0, ITERS, refine, both)
     x_ref[...] = both[:, BLK:].astype(BF16)
+    store = pltpu.make_async_copy(x_ref, x_hbm, sem.at[0])
+    store.start()
+    store.wait()
 
 
 def newton(token_total, packed, extra):
+    out = jax.ShapeDtypeStruct((BLK, BLK), BF16)
     return pl.pallas_call(
         lambda *refs: newton_kernel(token_total, *refs),
-        out_shape=jax.ShapeDtypeStruct((BLK, BLK), BF16),
-        in_specs=[pl.BlockSpec(memory_space=pltpu.VMEM)] * 2,
-        out_specs=pl.BlockSpec(memory_space=pltpu.VMEM),
-        cost_estimate=pl.CostEstimate(flops=2 * 14 * 6 * 2 * BLK**3, bytes_accessed=2**17, transcendentals=0),
+        out_shape=out,
+        in_specs=[pl.BlockSpec(memory_space=pl.ANY)] * 2,
+        out_specs=pl.BlockSpec(memory_space=pl.ANY),
+        scratch_shapes=[pltpu.VMEM(a.shape, a.dtype) for a in (packed, extra, out)] + [pltpu.SemaphoreType.DMA((2,))],
+        compiler_params=pltpu.CompilerParams(vmem_limit_bytes=62 * 2**20),
         name="newton",
     )(packed, extra)
 
 
 def spread_kernel(inv, owner_a, owner_g, r4, r5,
-                  p0, kept, s4, s_0, r_0, s_z, r_z, s_k, r_k, s_4, r_4, s_5, r_5):
+                  kept, es, er, s4, s_l, s_p, r_p, s_z, r_z, s_q, r_q, s_e, r_e, s_4, r_4, s_5, r_5):
     x, y, z, c = place()
-    yh, yl = y // NYL, y % NYL
-    dp, own = lax.axis_index("dp"), lax.axis_index("own")
-    e = 2 * x + yh
+    own = lax.axis_index("own")
+    yh, q = y // NYL, y % 2
     sib = device(x, y, z, 1 - c)
-
-    def peer(j):
-        other = (e + j) % 8
-        return other, device(other // 2, (other % 2) * NYL + yl, z, c)
 
     barrier = pltpu.get_barrier_semaphore()
     pl.semaphore_signal(barrier, inc=1, device_id=sib, device_id_type=MESH)
-    for j in range(1, 8):
-        pl.semaphore_signal(barrier, inc=1, device_id=peer(j)[1], device_id_type=MESH)
+    for j in range(1, NX):
+        pl.semaphore_signal(barrier, inc=1, device_id=device((x + j) % NX, y, z, c), device_id_type=MESH)
+    for step in (1, NY - 1):
+        pl.semaphore_signal(barrier, inc=1, device_id=device(x, (y + step) % NY, z, c), device_id_type=MESH)
     for j in range(1, NZ):
         pl.semaphore_signal(barrier, inc=1, device_id=device(x, y, (z + j) % NZ, c), device_id_type=MESH)
+
+    mine_here = pltpu.make_async_copy(inv.at[pl.ds(pl.multiple_of(32 * x, 32), 32)], kept.at[q, z, x], s_l)
+    mine_here.start()
 
     def find_a(b, found):
         at = owner_a[b] - 3 * own
@@ -361,110 +371,160 @@
     slot_g = lax.fori_loop(0, 32, find_g, zero)
 
     def at_a(b):
-        return b // 48, (b % 48) // 6, b % 6
+        return b % 2, (b % 48) // 6, (b % 6) // 2
 
     def at_g(b):
-        return b // 16, (b % 16) // 2, 6 + b % 2
-
-    want = [tuple(jnp.where(c == 0, s, n) for s, n in zip(at_a(slot_a[k]), at_a(3 * own + k))) for k in range(3)]
-    want.append(at_g(slot_g))
-
-    pl.semaphore_wait(barrier, 1 + 7 + (NZ - 1))
-
-    for j in range(1, 8):
-        other, to = peer(j)
-        send(inv.at[pl.ds(pl.multiple_of(16 * other, 16), 16)], p0.at[e], s_0.at[j - 1], r_0.at[j - 1], to)
-    p0[e] = inv[pl.ds(pl.multiple_of(16 * e, 16), 16), :]
-    for j in range(1, 8):
-        arrived(p0.at[(e - j + 8) % 8], r_0.at[j - 1])
+        return b % 2, (b % 16) // 2, 3
+
+    def entry(core, k):
+        if k == 3:
+            return slot_g // 16, at_g(slot_g)
+        block = jnp.where(core == 0, slot_a[k], 3 * own + k)
+        return block // 48, at_a(block)
+
+    mine = [entry(c, k) for k in range(4)]
+    theirs = [entry(1 - c, k) for k in range(4)]
+    mine_here.wait()
+    pl.semaphore_wait(barrier, 1 + (NX - 1) + 2 + (NZ - 1))
+
+    for j in range(1, NX):
+        to = (x + j) % NX
+        send(inv.at[pl.ds(pl.multiple_of(32 * to, 32), 32)], kept.at[q, z, x],
+             s_p.at[j - 1], r_p.at[j - 1], device(to, y, z, c))
+    for j in range(1, NX):
+        arrived(kept.at[q, z, (x - j + NX) % NX], r_p.at[j - 1])
     for j in range(1, NZ):
-        send(p0, kept.at[c, z], s_z.at[j - 1], r_z.at[j - 1], device(x, y, (z + j) % NZ, c))
-    send(p0, kept.at[c, z], s_k.at[0], r_k.at[0], sib)
-    kept[c, z] = p0[...]
+        send(kept.at[q, z], kept.at[q, z], s_z.at[j - 1], r_z.at[j - 1], device(x, y, (z + j) % NZ, c))
+
+    def to_neighbours(zz, j):
+        for k, step in enumerate((1, NY - 1)):
+            half = kept.at[q, zz, pl.ds(2 * k, 2)]
+            send(half, half, s_q.at[j, k], r_q.at[j, k], device(x, (y + step) % NY, z, c))
+
+    to_neighbours(z, 0)
     for j in range(1, NZ):
         zz = (z - j + NZ) % NZ
-        arrived(kept.at[c, zz], r_z.at[j - 1])
-        send(kept.at[c, zz], kept.at[c, zz], s_k.at[j], r_k.at[j], sib)
+        arrived(kept.at[q, zz], r_z.at[j - 1])
+        to_neighbours(zz, j)
     for j in range(NZ):
-        arrived(kept.at[1 - c, (z - j + NZ) % NZ], r_k.at[j])
-
-    shared = [kept[w] for w in want]
-    for j in range(1, 9):
-        other, to = peer(j)
+        zz = (z - j + NZ) % NZ
+        for k in range(2):
+            arrived(kept.at[1 - q, zz, pl.ds(2 * k, 2)], r_q.at[j, k])
+
+    for k in range(4):
+        es[k] = kept[theirs[k][1]]
+    for m in range(2):
+        for k in range(2):
+            es[4 + 2 * m + k] = kept[at_g(8 * (2 * c + m) + 4 * yh + 2 * (1 - c) + k)]
+    send(es, er, s_e.at[0], r_e.at[0], sib)
+    values = [kept[mine[k][1]] for k in range(4)]
+    arrived(er, r_e.at[0])
+    values = [jnp.where(mine[k][0] == c, values[k], er[k]) for k in range(4)]
+    for j in range(1, NX + 1):
+        to = (x + j) % NX
         for k in range(4):
-            s4[other, k] = shared[k]
+            s4[to, k] = values[k]
         for k in range(2):
-            s4[other, 4 + k] = kept[at_g(2 * (2 * other + c) + k)]
-        if j < 8:
-            send(s4.at[other], r4.at[e], s_4.at[j - 1], r_4.at[j - 1], to)
-    r4[e] = s4[e]
-    send(s4.at[e, pl.ds(0, 4)], r5.at[e], s_5.at[0], r_5.at[0], sib)
-    for j in range(1, 8):
-        other = (e - j + 8) % 8
-        arrived(r4.at[other], r_4.at[j - 1])
-        send(r4.at[other, pl.ds(0, 4)], r5.at[other], s_5.at[j], r_5.at[j], sib)
-    for j in range(8):
-        arrived(r5.at[(e - j + 8) % 8], r_5.at[j])
-
-    for j in range(7):
-        arrived(p0.at[0], s_0.at[j])
-        arrived(p0, s_z.at[j])
-        arrived(s4.at[0], s_4.at[j])
-    for j in range(8):
-        arrived(p0, s_k.at[j])
-        arrived(r5.at[0], s_5.at[j])
+            here = kept[at_g(8 * to + 4 * yh + 2 * c + k)]
+            s4[to, 4 + k] = jnp.where(to // 2 == c, here, er[4 + 2 * (to % 2) + k])
+        if j < NX:
+            send(s4.at[to], r4.at[x], s_4.at[j - 1], r_4.at[j - 1], device(to, y, z, c))
+    r4[x] = s4[x]
+    send(s4.at[x, pl.ds(0, 4)], r5.at[x], s_5.at[0], r_5.at[0], sib)
+    for j in range(1, NX):
+        frm = (x - j + NX) % NX
+        arrived(r4.at[frm], r_4.at[j - 1])
+        send(r4.at[frm, pl.ds(0, 4)], r5.at[frm], s_5.at[j], r_5.at[j], sib)
+    for j in range(NX):
+        arrived(r5.at[(x - j + NX) % NX], r_5.at[j])
+
+    for j in range(NZ):
+        for k in range(2):
+            arrived(kept.at[q, j, pl.ds(2 * k, 2)], s_q.at[j, k])
+    for j in range(NZ - 1):
+        arrived(kept.at[q, z], s_z.at[j])
+    for j in range(NX - 1):
+        arrived(kept.at[q, z, x], s_p.at[j])
+        arrived(s4.at[j], s_4.at[j])
+    arrived(es, s_e.at[0])
+    for j in range(NX):
+        arrived(r5.at[j], s_5.at[j])
 
 
 def spread(inv, owner_a, owner_g):
     dma = pltpu.SemaphoreType.DMA
     vm = pltpu.VMEM
-    piece = (16, BLK)
+    piece = (32, BLK)
+    shapes = ((NX - 1,), (NZ - 1,), (NZ, 2), (1,), (NX - 1,), (NX,))
     return pl.pallas_call(
         spread_kernel,
-        out_shape=(jax.ShapeDtypeStruct((8, 6) + piece, BF16), jax.ShapeDtypeStruct((8, 4) + piece, BF16)),
-        in_specs=[pl.BlockSpec(memory_space=pltpu.VMEM)] + [pl.BlockSpec(memory_space=pltpu.SMEM)] * 2,
+        out_shape=(jax.ShapeDtypeStruct((NX, 6) + piece, BF16), jax.ShapeDtypeStruct((NX, 4) + piece, BF16)),
+        in_specs=[pl.BlockSpec(memory_space=pl.ANY)] + [pl.BlockSpec(memory_space=pltpu.SMEM)] * 2,
         out_specs=[pl.BlockSpec(memory_space=pltpu.VMEM)] * 2,
         scratch_shapes=[
-            vm((8,) + piece, BF16), vm((2, NZ, 8) + piece, BF16), vm((8, 6) + piece, BF16),
-            dma((7,)), dma((7,)), dma((7,)), dma((7,)), dma((8,)), dma((8,)),
-            dma((7,)), dma((7,)), dma((8,)), dma((8,)),
-        ],
+            vm((2, NZ, NX) + piece, BF16), vm((8,) + piece, BF16), vm((8,) + piece, BF16), vm((NX, 6) + piece, BF16), dma,
+        ] + [dma(shape) for shape in shapes for _ in range(2)],
         compiler_params=pltpu.CompilerParams(
-            collective_id=1, has_side_effects=True, vmem_limit_bytes=16 * 2**20
+            collective_id=1, has_side_effects=True, vmem_limit_bytes=62 * 2**20
         ),
         name="spread_inverses",
     )(inv, owner_a, owner_g)
 
 
-def apply_kernel(r4, r5, w, a_out, g_out, p_out):
+def apply_kernel(r4_hbm, r5_hbm, w_hbm, a_hbm, g_hbm, p_hbm, r4, r5, w, a_out, g_out, p_out, s_in, s_out):
     _, _, _, c = place()
+    loads = [
+        pltpu.make_async_copy(src, dst, s_in.at[k])
+        for k, (src, dst) in enumerate(((r4_hbm, r4), (r5_hbm, r5), (w_hbm, w)))
+    ]
+    for load in loads:
+        load.start()
+    for load in loads:
+        load.wait()
 
     def whole(ref, k):
         return ref[:, k].reshape(BLK, BLK)
 
     mine = [whole(r4, k) for k in range(6)]
     theirs = [whole(r5, k) for k in range(4)]
-    even = c == 0
+    core0 = c == 0
+    stores = []
+
+    def store(src, dst):
+        stores.append(pltpu.make_async_copy(src, dst, s_out.at[len(stores)]))
+        stores[-1].start()
+
     for k in range(3):
-        a_out[k] = jnp.where(even, mine[k], theirs[k])
-    g_out[0] = mine[3]
-    for k in range(3):
-        nat = jnp.where(even, theirs[k], mine[k])
+        placed = jnp.where(core0, theirs[k], mine[k])
         rows = pl.ds(BLK * k, BLK)
-        left = jnp.dot(nat, w[rows, :], preferred_element_type=F32).astype(BF16)
+        left = jnp.dot(placed, w[rows, :], preferred_element_type=F32).astype(BF16)
         for m in range(2):
             cols = slice(BLK * m, BLK * (m + 1))
             p_out[rows, cols] = jnp.dot(left[:, cols], mine[4 + m], preferred_element_type=F32)
+        store(p_out.at[rows], p_hbm.at[rows])
+    for k in range(3):
+        a_out[k] = jnp.where(core0, mine[k], theirs[k])
+    store(a_out, a_hbm)
+    g_out[0] = mine[3]
+    store(g_out, g_hbm)
+    for each in stores:
+        each.wait()
 
 
 def apply_inverses(r4, r5, w):
+    outs = (
+        jax.ShapeDtypeStruct((3, BLK, BLK), BF16),
+        jax.ShapeDtypeStruct((1, BLK, BLK), BF16),
+        jax.ShapeDtypeStruct(w.shape, F32),
+    )
     return pl.pallas_call(
         apply_kernel,
-        out_shape=(
-            jax.ShapeDtypeStruct((3, BLK, BLK), BF16),
-            jax.ShapeDtypeStruct((1, BLK, BLK), BF16),
-            jax.ShapeDtypeStruct(w.shape, F32),
-        ),
+        out_shape=outs,
+        in_specs=[pl.BlockSpec(memory_space=pl.ANY)] * 3,
+        out_specs=[pl.BlockSpec(memory_space=pl.ANY)] * 3,
+        scratch_shapes=[pltpu.VMEM(a.shape, a.dtype) for a in (r4, r5, w) + outs]
+        + [pltpu.SemaphoreType.DMA((3,)), pltpu.SemaphoreType.DMA((5,))],
+        compiler_params=pltpu.CompilerParams(vmem_limit_bytes=62 * 2**20),
         name="apply_inverses",
     )(r4, r5, w)
 

time: 92.2 us -> 85.4 us (0.926)
  local copies, waits for them, and re-layouts: 6.4 us -> 0 us
    unnamed x18 -> x0, local copies, waits for them, and re-layouts: 6.4 us -> none
where the time goes in v2:
time: 85.4 us; the launch traced here: 85.2 us
  Pallas kernels  84.5 us (99%)
    pallas_call x1, Pallas kernels, gram_sums(): pl.pallas_call(gram_kernel, out_shape=(jax.ShapeDtypeStruct((NY, 2) + til...  50.5 us
    pallas_call x1, Pallas kernels, spread(): pl.pallas_call(spread_kernel, out_shape=(jax.ShapeDtypeStruct((NX, 6) + p...  27 us
    pallas_call x1, Pallas kernels, newton(): pl.pallas_call(lambda *refs: newton_kernel(token_total, *refs), out_shape...  4.77 us
    pallas_call x1, Pallas kernels, apply_inverses(): pl.pallas_call(apply_kernel, out_shape=outs, in_specs=[pl.BlockSpec(memor...  2.23 us

profile of v2, /device:TPU:1, one launch (start us, length us, event | category | flops | bytes accessed | tf_op | source)
XLA Modules:
  0.0 85.2 jit_solution(5220518383764863440)
XLA Ops:
  0.6 50.5 %gram_sums.1 = (f32[8,2,8,128]{3,2,1,0:T(8,128)}, f32[8,128]{1,0:T(8,128)}) custom-call(bf16[128,12288]{1,0:T(8,128)(2,1)} %hid.1, bf16[128,4096]{1,0:T(8,128)(2,1)} %grd.1), custom_call_target="tpu_custom_call" | custom-call | flops 536870912 | bytes 4194304 | tf_op jit(solution)/shard_map/gram_sums/pallas_call | solution.py:236
  51.1 4.8 %newton.1.inv = bf16[128,128]{1,0:T(8,128)(2,1)} custom-call(f32[8,2,8,128]{3,2,1,0:T(8,128)} %get-tuple-element.7.refs_0_, f32[8,128]{1,0:T(8,128)} %get-tuple-element.8.refs_1_), custom_call_target="tpu_custom_call" | custom-call | tf_op jit(solution)/shard_map/newton/pallas_call | solution.py:332
  55.9 27.0 %spread_inverses.1 = (bf16[4,6,32,128]{3,2,1,0:T(8,128)(2,1)}, bf16[4,4,32,128]{3,2,1,0:T(8,128)(2,1)}) custom-call(bf16[128,128]{1,0:T(8,128)(2,1)} %newton.1.inv, s32[96]{0:T(128)} %owner_a.1, s32[32]{0:T(128)} %owner_g.1), custom_call_target="tpu_custom_call" | custom-call | tf_op jit(solution)/shard_map/spread_inverses/pallas_call | solution.py:459
  82.9 2.2 %apply_inverses.1 = (bf16[3,128,128]{2,1,0:T(8,128)(2,1)}, bf16[1,128,128]{2,1,0:T(8,128)(2,1)}, f32[384,256]{1,0:T(8,128)}) custom-call(bf16[4,6,32,128]{3,2,1,0:T(8,128)(2,1)} %get-tuple-element.9.r4_hbm, bf16[4,4,32,128]{3,2,1,0:T(8,128)(2,1)} %get-tuple-element.10.r5_hbm, bf16[384,256]{1,0:T(8,128)(2,1)} %w_hbm.1), custom_call_target="tpu_custom_call" | custom-call | tf_op jit(solution)/shard_map/apply_inverses/pallas_call | solution.py:520

commit v3 on v2

v3 whole, which is shorter than its diff:
```python
import jax
import jax.numpy as jnp
from jax import lax
from jax.experimental import pallas as pl
from jax.experimental.pallas import tpu as pltpu
from jax.sharding import PartitionSpec as P

BLK = 128
ITERS = 14
FINE = 4
DAMPING = 0.05
NX, NY, NZ, NYL = 4, 8, 8, 4
MESH = pl.DeviceIdType.MESH
F32 = jnp.float32
BF16 = jnp.bfloat16


def place():
    dp = lax.axis_index("dp")
    own = lax.axis_index("own")
    return dp // 4, ((dp // 2) % 2) * NYL + own % NYL, own // NYL, dp % 2


def device(x, y, z, c):
    return (x * 4 + (y // NYL) * 2 + c, z * NYL + y % NYL)


def send(src, dst, send_sem, recv_sem, to):
    copy = pltpu.make_async_remote_copy(
        src_ref=src, dst_ref=dst, send_sem=send_sem, recv_sem=recv_sem,
        device_id=to, device_id_type=MESH,
    )
    copy.start()


def arrived(ref, sem):
    pltpu.make_async_copy(ref, ref, sem).wait()


def gram_kernel(hid, grd, m_out, d_out,
                raw, ta, tg, ra, rz, rg, rx, a3, r3, fin,
                s_loc, s_raw_s, s_raw_r, s_a, r_a, s_z, r_z, s_g, r_g, s_x, r_x, s_3, r_3, s_f, r_f):
    x, y, z, c = place()
    sib = device(x, y, z, 1 - c)

    barrier = pltpu.get_barrier_semaphore()
    pl.semaphore_signal(barrier, inc=1, device_id=sib, device_id_type=MESH)
    for j in range(1, NX):
        pl.semaphore_signal(barrier, inc=1, device_id=device((x + j) % NX, y, z, c), device_id_type=MESH)
    for j in range(1, NY):
        pl.semaphore_signal(barrier, inc=1, device_id=device(x, (y + j) % NY, z, c), device_id_type=MESH)
    for j in (1, NZ - 1):
        pl.semaphore_signal(barrier, inc=1, device_id=device(x, y, (z + j) % NZ, c), device_id_type=MESH)

    def target(i):
        return (z + 4 + (2 * (i % 2) - 1) * ((i + 1) // 2)) % NZ

    def onward(i):
        return device(x, y, (z + NZ + 1 - 2 * (i % 2)) % NZ, c)

    def parts(zz, core, rows):
        return (
            (hid.at[:, pl.ds(pl.multiple_of(6144 * core + 768 * zz, 128), 768)],
             raw.at[rows, pl.ds(pl.multiple_of(1024 * zz, 128), 768)]),
            (grd.at[:, pl.ds(pl.multiple_of(2048 * core + 256 * zz, 128), 256)],
             raw.at[rows, pl.ds(pl.multiple_of(1024 * zz + 768, 128), 256)]),
        )

    low, high = pl.ds(0, 128), pl.ds(128, 128)

    @pl.loop(0, NZ)
    def _(i):
        for k, (src, dst) in enumerate(parts(target(i), c, low)):
            pltpu.make_async_copy(src, dst, s_loc.at[i, k]).start()

    pl.semaphore_wait(barrier, 1 + (NX - 1) + (NY - 1) + 2)

    @pl.loop(0, NZ)
    def _(i):
        for k, (src, dst) in enumerate(parts(target(i), 1 - c, high)):
            send(src, dst, s_raw_s.at[i, k], s_raw_r.at[i, k], sib)

    row8 = lax.broadcasted_iota(jnp.int32, (BLK, BLK), 0) // 8
    col8 = lax.broadcasted_iota(jnp.int32, (BLK, BLK), 1) // 8
    upper = row8 <= col8
    middle = row8 == col8

    def gram(zz, k):
        cols = pl.ds(pl.multiple_of(1024 * zz + BLK * k, BLK), BLK)
        tok = raw[:, cols]
        return lax.dot_general(tok, tok, (((0,), (0,)), ((), ())), preferred_element_type=F32)

    def gram_step(i, first, last):
        zz = target(i)
        for k, (src, dst) in enumerate(parts(zz, c, low)):
            pltpu.make_async_copy(src, dst, s_loc.at[i, k]).wait()
        for k, (src, dst) in enumerate(parts(zz, c, high)):
            arrived(dst, s_raw_r.at[i, k])
        for xx in range(NX):
            one = gram(zz, 2 * xx)
            two = gram(zz, 2 * xx + 1)
            packed = jnp.where(upper, one, two).reshape(NY, 2, 8, BLK)
            extra = jnp.sum(jnp.where(middle, two, 0.0).reshape(16, 8, BLK), axis=0)
            ta[zz, xx, pl.ds(0, NY)] = packed[:, 0]
            ta[zz, xx, NY] = extra
            tile1 = packed[:, 1]
            if not first:
                arrived(rg.at[i - 2, xx], r_g.at[i - 2, xx])
                tile1 = tile1 + rg[i - 2, xx]
            if last:
                arrived(rg.at[i - 1, xx], r_g.at[i - 1, xx])
                tile1 = tile1 + rg[i - 1, xx]
            tg[zz, xx] = tile1
            if not last:
                send(tg.at[zz, xx], rg.at[i, xx], s_g.at[i, xx], r_g.at[i, xx], onward(i))
        for j in range(1, NX):
            to = (x + j) % NX
            send(ta.at[zz, to], ra.at[j - 1, zz], s_a.at[j - 1, i], r_a.at[j - 1, i], device(to, y, z, c))

    def tile0_step(i, first, last):
        zz = target(i)
        total = ta[zz, x]
        for j in range(NX - 1):
            arrived(ra.at[j, zz], r_a.at[j, i])
            total = total + ra[j, zz]
        if not first:
            arrived(rz.at[i - 2], r_z.at[i - 2])
            total = total + rz[i - 2]
        if last:
            arrived(rz.at[i - 1], r_z.at[i - 1])
            total = total + rz[i - 1]
        else:
            ta[zz, x] = total
            send(ta.at[zz, x], rz.at[i], s_z.at[i], r_z.at[i], onward(i))
        return total

    @pl.loop(0, 2)
    def _(i):
        gram_step(i, True, False)

    @pl.loop(2, 4)
    def _(i):
        gram_step(i, False, False)
        tile0_step(i - 2, True, False)

    @pl.loop(4, 7)
    def _(i):
        gram_step(i, False, False)
        tile0_step(i - 2, False, False)

    gram_step(7, False, True)
    for j in range(1, NX):
        to = (x + j) % NX
        send(tg.at[z, to], rx.at[j - 1], s_x.at[j - 1], r_x.at[j - 1], device(to, y, z, c))
    tile0_step(5, False, False)
    tile0_step(6, False, False)
    total0 = tile0_step(7, False, True)
    total1 = tg[z, x]
    for j in range(NX - 1):
        arrived(rx.at[j], r_x.at[j])
        total1 = total1 + rx[j]

    for yy in range(NY):
        a3[yy, 0] = total0[yy]
        a3[yy, 1] = total1[yy]
        a3[yy, 2] = total0[NY]
    for j in range(1, NY):
        to = (y + j) % NY
        send(a3.at[to], r3.at[j - 1], s_3.at[j - 1], r_3.at[j - 1], device(x, to, z, c))
    total = a3[y]
    for j in range(NY - 1):
        arrived(r3.at[j], r_3.at[j])
        total = total + r3[j]
    fin[...] = total[:2]
    d_out[...] = total[2]

    m_out[y] = total[:2]
    for j in range(1, NY):
        to = (y + j) % NY
        send(fin, m_out.at[y], s_f.at[j - 1], r_f.at[j - 1], device(x, to, z, c))
    for j in range(1, NY):
        arrived(m_out.at[(y - j + NY) % NY], r_f.at[j - 1])

    @pl.loop(0, NZ)
    def _(i):
        for k, (src, dst) in enumerate(parts(target(i), 1 - c, high)):
            arrived(src, s_raw_s.at[i, k])
        for j in range(NX - 1):
            arrived(ta.at[0, 0], s_a.at[j, i])

    @pl.loop(0, NZ - 1)
    def _(i):
        for xx in range(NX):
            arrived(tg.at[0, 0], s_g.at[i, xx])
        arrived(ta.at[0, 0], s_z.at[i])
        arrived(a3.at[0], s_3.at[i])
        arrived(fin, s_f.at[i])

    for j in range(NX - 1):
        arrived(tg.at[0, 0], s_x.at[j])


def gram_sums(hid, grd):
    dma = pltpu.SemaphoreType.DMA
    tile = (8, BLK)
    vm = pltpu.VMEM
    shapes = ((NZ, 2), (NX - 1, NZ), (NZ - 1,), (NZ - 1, NX), (NX - 1,), (NY - 1,), (NY - 1,))
    return pl.pallas_call(
        gram_kernel,
        out_shape=(jax.ShapeDtypeStruct((NY, 2) + tile, F32), jax.ShapeDtypeStruct(tile, F32)),
        in_specs=[pl.BlockSpec(memory_space=pl.ANY)] * 2,
        out_specs=[pl.BlockSpec(memory_space=pltpu.VMEM)] * 2,
        scratch_shapes=[
            vm((256, 8192), BF16),
            vm((NZ, NX, NY + 1) + tile, F32),
            vm((NZ, NX, NY) + tile, F32),
            vm((NX - 1, NZ, NY + 1) + tile, F32),
            vm((NZ - 1, NY + 1) + tile, F32),
            vm((NZ - 1, NX, NY) + tile, F32),
            vm((NX - 1, NY) + tile, F32),
            vm((NY, 3) + tile, F32),
            vm((NY - 1, 3) + tile, F32),
            vm((2,) + tile, F32),
            dma((NZ, 2)),
        ] + [dma(shape) for shape in shapes for _ in range(2)],
        compiler_params=pltpu.CompilerParams(
            collective_id=0, has_side_effects=True, vmem_limit_bytes=62 * 2**20
        ),
        cost_estimate=pl.CostEstimate(flops=2 * 64 * 256 * BLK * BLK, bytes_accessed=4 * 2**20, transcendentals=0),
        name="gram_sums",
    )(hid, grd)


def split3(value):
    high = value.astype(BF16)
    rest = value - high.astype(F32)
    mid = rest.astype(BF16)
    return high, mid, (rest - mid.astype(F32)).astype(BF16)


def product(left, right, fine):
    lh, lm, ll = split3(left)
    rh, rm, rl = split3(right)

    def dot(a, b):
        return jnp.dot(a, b, preferred_element_type=F32)

    if not fine:
        return dot(jnp.concatenate((lh, lm), axis=1), jnp.concatenate((rh, rh), axis=0)) + dot(lh, rm)
    small = dot(jnp.concatenate((lm, ll), axis=1), jnp.concatenate((rm, rh), axis=0))
    middle = dot(jnp.concatenate((lh, lm), axis=1), jnp.concatenate((rm, rh), axis=0))
    large = dot(jnp.concatenate((lh, lh), axis=1), jnp.concatenate((rh, rl), axis=0))
    return large + (middle + small)


def newton_kernel(token_total, m_hbm, d_hbm, x_hbm, m_ref, d_ref, x_ref, sem):
    loads = [pltpu.make_async_copy(m_hbm, m_ref, sem.at[0]), pltpu.make_async_copy(d_hbm, d_ref, sem.at[1])]
    for load in loads:
        load.start()
    for load in loads:
        load.wait()
    _, y, _, _ = place()
    second = (y % 2) == 1
    packed = m_ref[...].reshape(BLK, BLK)
    extra = jnp.broadcast_to(d_ref[...][None], (16, 8, BLK)).reshape(BLK, BLK)
    row = lax.broadcasted_iota(jnp.int32, (BLK, BLK), 0)
    col = lax.broadcasted_iota(jnp.int32, (BLK, BLK), 1)
    turned = packed.T
    first_block = jnp.where(row // 8 <= col // 8, packed, turned)
    second_block = jnp.where(row // 8 == col // 8, extra, jnp.where(row // 8 > col // 8, packed, turned))
    sums = jnp.where(second, second_block, first_block)
    identity = jnp.where(row == col, 1.0, 0.0)
    factor = sums / token_total + DAMPING * identity
    bound = jnp.max(jnp.sum(jnp.abs(factor), axis=1, keepdims=True), axis=0, keepdims=True)
    both = jnp.concatenate((factor / bound, identity / bound), axis=1)

    def refine(fine):
        return lambda step, both: 2.0 * both - product(both[:, :BLK], both, fine)

    both = lax.fori_loop(0, FINE, refine(True), both)
    both = lax.fori_loop(FINE, ITERS, refine(False), both)
    x_ref[...] = both[:, BLK:].astype(BF16)
    store = pltpu.make_async_copy(x_ref, x_hbm, sem.at[0])
    store.start()
    store.wait()


def newton(token_total, packed, extra):
    out = jax.ShapeDtypeStruct((BLK, BLK), BF16)
    return pl.pallas_call(
        lambda *refs: newton_kernel(token_total, *refs),
        out_shape=out,
        in_specs=[pl.BlockSpec(memory_space=pl.ANY)] * 2,
        out_specs=pl.BlockSpec(memory_space=pl.ANY),
        scratch_shapes=[pltpu.VMEM(a.shape, a.dtype) for a in (packed, extra, out)] + [pltpu.SemaphoreType.DMA((2,))],
        compiler_params=pltpu.CompilerParams(vmem_limit_bytes=62 * 2**20),
        name="newton",
    )(packed, extra)


def spread_kernel(inv, owner_a, owner_g, r4, rg, r5,
                  kept, sh, sg, s_l, s_p, r_p, s_z, r_z, s_k, r_k, s_q, r_q, s_4, r_4, s_g, r_g, s_5, r_5):
    x, y, z, c = place()
    own = lax.axis_index("own")
    yh, q = y // NYL, y % 2
    sib = device(x, y, z, 1 - c)
    beside = [device(x, (y + step) % NY, z, core) for core in (c, 1 - c) for step in (1, NY - 1)]

    barrier = pltpu.get_barrier_semaphore()
    for to in [sib] + beside:
        pl.semaphore_signal(barrier, inc=1, device_id=to, device_id_type=MESH)
    for j in range(1, NX):
        for core in (c, 1 - c):
            pl.semaphore_signal(barrier, inc=1, device_id=device((x + j) % NX, y, z, core), device_id_type=MESH)
    for j in range(1, NZ):
        pl.semaphore_signal(barrier, inc=1, device_id=device(x, y, (z + j) % NZ, c), device_id_type=MESH)

    mine_here = pltpu.make_async_copy(inv.at[pl.ds(pl.multiple_of(32 * x, 32), 32)], kept.at[c, q, z, x], s_l)
    mine_here.start()

    def find_a(b, found):
        at = owner_a[b] - 3 * own
        return tuple(jnp.where(at == k, b, found[k]) for k in range(3))

    def find_g(b, found):
        return jnp.where(owner_g[b] == own, b, found)

    zero = jnp.int32(0)
    slot_a = lax.fori_loop(0, 96, find_a, (zero, zero, zero))
    slot_g = lax.fori_loop(0, 32, find_g, zero)

    def at_a(b):
        return b // 48, b % 2, (b % 48) // 6, (b % 6) // 2

    def at_g(b):
        return b // 16, b % 2, (b % 16) // 2, 3

    want = [at_a(jnp.where(c == 0, slot_a[k], 3 * own + k)) for k in range(3)] + [at_g(slot_g)]
    mine_here.wait()
    pl.semaphore_wait(barrier, 5 + 2 * (NX - 1) + (NZ - 1))

    for j in range(1, NX):
        to = (x + j) % NX
        send(inv.at[pl.ds(pl.multiple_of(32 * to, 32), 32)], kept.at[c, q, z, x],
             s_p.at[j - 1], r_p.at[j - 1], device(to, y, z, c))
    for j in range(1, NX):
        arrived(kept.at[c, q, z, (x - j + NX) % NX], r_p.at[j - 1])
    for j in range(1, NZ):
        send(kept.at[c, q, z], kept.at[c, q, z], s_z.at[j - 1], r_z.at[j - 1], device(x, y, (z + j) % NZ, c))

    def pass_on(zz, j):
        for k in range(4):
            half = kept.at[c, q, zz, pl.ds(2 * (k % 2), 2)]
            send(half, half, s_q.at[j, k], r_q.at[j, k], beside[k])
        send(kept.at[c, q, zz], kept.at[c, q, zz], s_k.at[j], r_k.at[j], sib)

    pass_on(z, 0)
    for j in range(1, NZ):
        zz = (z - j + NZ) % NZ
        arrived(kept.at[c, q, zz], r_z.at[j - 1])
        pass_on(zz, j)
    for j in range(NZ):
        zz = (z - j + NZ) % NZ
        arrived(kept.at[1 - c, q, zz], r_k.at[j])
        for k in range(4):
            arrived(kept.at[(c + k // 2) % 2, 1 - q, zz, pl.ds(2 * (k % 2), 2)], r_q.at[j, k])

    for k in range(4):
        sh[k] = kept[want[k]]
    for j in range(1, NX + 1):
        to = (x + j) % NX
        for k in range(2):
            sg[to, k] = kept[at_g(8 * to + 4 * yh + 2 * c + k)]
        if j < NX:
            send(sh, r4.at[x], s_4.at[j - 1], r_4.at[j - 1], device(to, y, z, c))
            send(sh, r5.at[x], s_5.at[j - 1], r_5.at[j - 1], device(to, y, z, 1 - c))
            send(sg.at[to], rg.at[x], s_g.at[j - 1], r_g.at[j - 1], device(to, y, z, c))
    send(sh, r5.at[x], s_5.at[NX - 1], r_5.at[NX - 1], sib)
    r4[x] = sh[...]
    rg[x] = sg[x]
    for j in range(1, NX):
        frm = (x - j + NX) % NX
        arrived(r4.at[frm], r_4.at[j - 1])
        arrived(rg.at[frm], r_g.at[j - 1])
        arrived(r5.at[frm], r_5.at[j - 1])
    arrived(r5.at[x], r_5.at[NX - 1])

    for j in range(NZ):
        for k in range(4):
            arrived(kept.at[c, q, j, pl.ds(0, 2)], s_q.at[j, k])
        arrived(kept.at[c, q, j], s_k.at[j])
    for j in range(NZ - 1):
        arrived(kept.at[c, q, z], s_z.at[j])
    for j in range(NX - 1):
        arrived(kept.at[c, q, z, x], s_p.at[j])
        arrived(sh, s_4.at[j])
        arrived(sg.at[0], s_g.at[j])
    for j in range(NX):
        arrived(sh, s_5.at[j])


def spread(inv, owner_a, owner_g):
    dma = pltpu.SemaphoreType.DMA
    vm = pltpu.VMEM
    piece = (32, BLK)
    shapes = ((NX - 1,), (NZ - 1,), (NZ,), (NZ, 4), (NX - 1,), (NX - 1,), (NX,))
    return pl.pallas_call(
        spread_kernel,
        out_shape=tuple(jax.ShapeDtypeStruct((NX, n) + piece, BF16) for n in (4, 2, 4)),
        in_specs=[pl.BlockSpec(memory_space=pl.ANY)] + [pl.BlockSpec(memory_space=pltpu.SMEM)] * 2,
        out_specs=[pl.BlockSpec(memory_space=pltpu.VMEM)] * 3,
        scratch_shapes=[vm((2, 2, NZ, NX) + piece, BF16), vm((4,) + piece, BF16), vm((NX, 2) + piece, BF16), dma]
        + [dma(shape) for shape in shapes for _ in range(2)],
        compiler_params=pltpu.CompilerParams(
            collective_id=1, has_side_effects=True, vmem_limit_bytes=62 * 2**20
        ),
        name="spread_inverses",
    )(inv, owner_a, owner_g)


def apply_kernel(r4_hbm, rg_hbm, r5_hbm, w_hbm, a_hbm, g_hbm, p_hbm, r4, rg, r5, w, a_out, g_out, p_out, s_in, s_out):
    _, _, _, c = place()
    loads = [
        pltpu.make_async_copy(src, dst, s_in.at[k])
        for k, (src, dst) in enumerate(((r4_hbm, r4), (rg_hbm, rg), (r5_hbm, r5), (w_hbm, w)))
    ]
    for load in loads:
        load.start()
    for load in loads:
        load.wait()

    def whole(ref, k):
        return ref[:, k].reshape(BLK, BLK)

    mine = [whole(r4, k) for k in range(4)]
    right = [whole(rg, k) for k in range(2)]
    theirs = [whole(r5, k) for k in range(4)]
    core0 = c == 0
    stores = []

    def store(src, dst):
        stores.append(pltpu.make_async_copy(src, dst, s_out.at[len(stores)]))
        stores[-1].start()

    for k in range(3):
        placed = jnp.where(core0, theirs[k], mine[k])
        rows = pl.ds(BLK * k, BLK)
        left = jnp.dot(placed, w[rows, :], preferred_element_type=F32).astype(BF16)
        for m in range(2):
            cols = slice(BLK * m, BLK * (m + 1))
            p_out[rows, cols] = jnp.dot(left[:, cols], right[m], preferred_element_type=F32)
        store(p_out.at[rows], p_hbm.at[rows])
    for k in range(3):
        a_out[k] = jnp.where(core0, mine[k], theirs[k])
    store(a_out, a_hbm)
    g_out[0] = mine[3]
    store(g_out, g_hbm)
    for each in stores:
        each.wait()


def apply_inverses(r4, rg, r5, w):
    outs = (
        jax.ShapeDtypeStruct((3, BLK, BLK), BF16),
        jax.ShapeDtypeStruct((1, BLK, BLK), BF16),
        jax.ShapeDtypeStruct(w.shape, F32),
    )
    return pl.pallas_call(
        apply_kernel,
        out_shape=outs,
        in_specs=[pl.BlockSpec(memory_space=pl.ANY)] * 4,
        out_specs=[pl.BlockSpec(memory_space=pl.ANY)] * 3,
        scratch_shapes=[pltpu.VMEM(a.shape, a.dtype) for a in (r4, rg, r5, w) + outs]
        + [pltpu.SemaphoreType.DMA((4,)), pltpu.SemaphoreType.DMA((5,))],
        compiler_params=pltpu.CompilerParams(vmem_limit_bytes=62 * 2**20),
        name="apply_inverses",
    )(r4, rg, r5, w)


def on_device(hidden_act, out_grad, weight_grad, owner_a, owner_g):
    token_total = hidden_act.shape[0] * lax.axis_size("own") * lax.axis_size("dp")
    packed, extra = gram_sums(hidden_act, out_grad)
    inverse = newton(token_total, packed, extra)
    return apply_inverses(*spread(inverse, owner_a, owner_g), weight_grad)


def solution(mesh):
    placed = (P(("dp", "own"), None), P(("dp", "own"), None), P("own", "dp"), P(), P())
    return jax.shard_map(
        on_device,
        mesh=mesh,
        in_specs=placed,
        out_specs=(P("own", None, None), P("own", None, None), P("own", "dp")),
        check_vma=False,
    )
```

time: 85.4 us -> 88.6 us (1.037)
  Pallas kernels: 84.5 us -> 87.7 us
    pallas_call x1, Pallas kernels: 27 us -> 30.5 us  [spread(): pl.pallas_call(spread_kernel, out_shape=tuple((jax.ShapeDtypeStruct((NX,...]
where the time goes in v3:
time: 88.6 us; the launch traced here: 88.4 us
  Pallas kernels  87.7 us (99%)
    pallas_call x1, Pallas kernels, gram_sums(): pl.pallas_call(gram_kernel, out_shape=(jax.ShapeDtypeStruct((NY, 2) + til...  50.6 us
    pallas_call x1, Pallas kernels, spread(): pl.pallas_call(spread_kernel, out_shape=tuple((jax.ShapeDtypeStruct((NX,...  30.5 us
    pallas_call x1, Pallas kernels, newton(): pl.pallas_call(lambda *refs: newton_kernel(token_total, *refs), out_shape...  4.39 us
    pallas_call x1, Pallas kernels, apply_inverses(): pl.pallas_call(apply_kernel, out_shape=outs, in_specs=[pl.BlockSpec(memor...  2.24 us

profile of v3, /device:TPU:1, one launch (start us, length us, event | category | flops | bytes accessed | tf_op | source)
XLA Modules:
  0.0 88.4 jit_solution(13680726691582137185)
XLA Ops:
  0.6 50.6 %gram_sums.1 = (f32[8,2,8,128]{3,2,1,0:T(8,128)}, f32[8,128]{1,0:T(8,128)}) custom-call(bf16[128,12288]{1,0:T(8,128)(2,1)} %hid.1, bf16[128,4096]{1,0:T(8,128)(2,1)} %grd.1), custom_call_target="tpu_custom_call" | custom-call | flops 536870912 | bytes 4194304 | tf_op jit(solution)/shard_map/gram_sums/pallas_call | solution.py:208
  51.2 4.4 %newton.1.inv = bf16[128,128]{1,0:T(8,128)(2,1)} custom-call(f32[8,2,8,128]{3,2,1,0:T(8,128)} %get-tuple-element.8.refs_0_, f32[8,128]{1,0:T(8,128)} %get-tuple-element.9.refs_1_), custom_call_target="tpu_custom_call" | custom-call | tf_op jit(solution)/shard_map/newton/pallas_call | solution.py:290
  55.6 30.5 %spread_inverses.1 = (bf16[4,4,32,128]{3,2,1,0:T(8,128)(2,1)}, bf16[4,2,32,128]{3,2,1,0:T(8,128)(2,1)}, bf16[4,4,32,128]{3,2,1,0:T(8,128)(2,1)}) custom-call(bf16[128,128]{1,0:T(8,128)(2,1)} %newton.1.inv, s32[96]{0:T(128)} %owner_a.1, s32[32]{0:T(128)} %owner_g.1), custom_call_target="tpu_custom_call" | custom-call | tf_op jit(solution)/shard_map/spread_inverses/pallas_call | solution.py:407
  86.1 2.2 %apply_inverses.1 = (bf16[3,128,128]{2,1,0:T(8,128)(2,1)}, bf16[1,128,128]{2,1,0:T(8,128)(2,1)}, f32[384,256]{1,0:T(8,128)}) custom-call(bf16[4,4,32,128]{3,2,1,0:T(8,128)(2,1)} %get-tuple-element.10.r4_hbm, bf16[4,2,32,128]{3,2,1,0:T(8,128)(2,1)} %get-tuple-element.11.rg_hbm, bf16[4,4,32,128]{3,2,1,0:T(8,128)(2,1)} %get-tuple-element.12.r5_hbm, ...), custom_call_target="tpu_custom_call" | custom-call | tf_op jit(solution)/shard_map/apply_inverses/pallas_call | solution.py:468

commit v4 on v3

--- a/solution.py
+++ b/solution.py
@@ -15,14 +15,32 @@
 BF16 = jnp.bfloat16
 
 
-def place():
-    dp = lax.axis_index("dp")
-    own = lax.axis_index("own")
-    return dp // 4, ((dp // 2) % 2) * NYL + own % NYL, own // NYL, dp % 2
-
-
-def device(x, y, z, c):
-    return (x * 4 + (y // NYL) * 2 + c, z * NYL + y % NYL)
+FAR_FIRST = (4, 3, 5, 2, 6, 1, 7)
+
+
+def mod(value, n):
+    return value % n if isinstance(value, int) else lax.rem(value, n)
+
+
+class Place:
+    def __init__(self):
+        self.dp, self.own = lax.axis_index("dp"), lax.axis_index("own")
+        self.x, self.c = lax.div(self.dp, 4), mod(self.dp, 2)
+        self.yh = mod(lax.div(self.dp, 2), 2)
+        self.z, self.yl = lax.div(self.own, NYL), mod(self.own, NYL)
+        self.y = self.yh * NYL + self.yl
+
+    def at_x(self, to):
+        return (self.dp + 4 * (to - self.x), self.own)
+
+    def at_y(self, to):
+        return (self.dp + 2 * (lax.div(to, NYL) - self.yh), self.own + mod(to, NYL) - self.yl)
+
+    def at_z(self, to):
+        return (self.dp, self.own + NYL * (to - self.z))
+
+    def other_core(self):
+        return (self.dp + 1 - 2 * self.c, self.own)
 
 
 def send(src, dst, send_sem, recv_sem, to):
@@ -40,23 +58,24 @@
 def gram_kernel(hid, grd, m_out, d_out,
                 raw, ta, tg, ra, rz, rg, rx, a3, r3, fin,
                 s_loc, s_raw_s, s_raw_r, s_a, r_a, s_z, r_z, s_g, r_g, s_x, r_x, s_3, r_3, s_f, r_f):
-    x, y, z, c = place()
-    sib = device(x, y, z, 1 - c)
+    here = Place()
+    x, y, z, c = here.x, here.y, here.z, here.c
+    sib = here.other_core()
 
     barrier = pltpu.get_barrier_semaphore()
     pl.semaphore_signal(barrier, inc=1, device_id=sib, device_id_type=MESH)
     for j in range(1, NX):
-        pl.semaphore_signal(barrier, inc=1, device_id=device((x + j) % NX, y, z, c), device_id_type=MESH)
+        pl.semaphore_signal(barrier, inc=1, device_id=here.at_x(mod(x + j, NX)), device_id_type=MESH)
     for j in range(1, NY):
-        pl.semaphore_signal(barrier, inc=1, device_id=device(x, (y + j) % NY, z, c), device_id_type=MESH)
+        pl.semaphore_signal(barrier, inc=1, device_id=here.at_y(mod(y + j, NY)), device_id_type=MESH)
     for j in (1, NZ - 1):
-        pl.semaphore_signal(barrier, inc=1, device_id=device(x, y, (z + j) % NZ, c), device_id_type=MESH)
+        pl.semaphore_signal(barrier, inc=1, device_id=here.at_z(mod(z + j, NZ)), device_id_type=MESH)
 
     def target(i):
-        return (z + 4 + (2 * (i % 2) - 1) * ((i + 1) // 2)) % NZ
+        return mod(z + 4 + (2 * mod(i, 2) - 1) * ((i + 1) // 2 if isinstance(i, int) else lax.div(i + 1, 2)), NZ)
 
     def onward(i):
-        return device(x, y, (z + NZ + 1 - 2 * (i % 2)) % NZ, c)
+        return here.at_z(mod(z + NZ + 1 - 2 * mod(i, 2), NZ))
 
     def parts(zz, core, rows):
         return (
@@ -103,19 +122,20 @@
             extra = jnp.sum(jnp.where(middle, two, 0.0).reshape(16, 8, BLK), axis=0)
             ta[zz, xx, pl.ds(0, NY)] = packed[:, 0]
             ta[zz, xx, NY] = extra
-            tile1 = packed[:, 1]
+            tg[zz, xx] = packed[:, 1]
+        for j in (2, 1, 3):
+            to = mod(x + j, NX)
+            send(ta.at[zz, to], ra.at[j - 1, zz], s_a.at[j - 1, i], r_a.at[j - 1, i], here.at_x(to))
+        for xx in range(NX):
             if not first:
                 arrived(rg.at[i - 2, xx], r_g.at[i - 2, xx])
-                tile1 = tile1 + rg[i - 2, xx]
-            if last:
-                arrived(rg.at[i - 1, xx], r_g.at[i - 1, xx])
-                tile1 = tile1 + rg[i - 1, xx]
-            tg[zz, xx] = tile1
+                tile1 = tg[zz, xx] + rg[i - 2, xx]
+                if last:
+                    arrived(rg.at[i - 1, xx], r_g.at[i - 1, xx])
+                    tile1 = tile1 + rg[i - 1, xx]
+                tg[zz, xx] = tile1
             if not last:
                 send(tg.at[zz, xx], rg.at[i, xx], s_g.at[i, xx], r_g.at[i, xx], onward(i))
-        for j in range(1, NX):
-            to = (x + j) % NX
-            send(ta.at[zz, to], ra.at[j - 1, zz], s_a.at[j - 1, i], r_a.at[j - 1, i], device(to, y, z, c))
 
     def tile0_step(i, first, last):
         zz = target(i)
@@ -149,9 +169,9 @@
         tile0_step(i - 2, False, False)
 
     gram_step(7, False, True)
-    for j in range(1, NX):
-        to = (x + j) % NX
-        send(tg.at[z, to], rx.at[j - 1], s_x.at[j - 1], r_x.at[j - 1], device(to, y, z, c))
+    for j in (2, 1, 3):
+        to = mod(x + j, NX)
+        send(tg.at[z, to], rx.at[j - 1], s_x.at[j - 1], r_x.at[j - 1], here.at_x(to))
     tile0_step(5, False, False)
     tile0_step(6, False, False)
     total0 = tile0_step(7, False, True)
@@ -164,9 +184,9 @@
         a3[yy, 0] = total0[yy]
         a3[yy, 1] = total1[yy]
         a3[yy, 2] = total0[NY]
-    for j in range(1, NY):
-        to = (y + j) % NY
-        send(a3.at[to], r3.at[j - 1], s_3.at[j - 1], r_3.at[j - 1], device(x, to, z, c))
+    for j in FAR_FIRST:
+        to = mod(y + j, NY)
+        send(a3.at[to], r3.at[j - 1], s_3.at[j - 1], r_3.at[j - 1], here.at_y(to))
     total = a3[y]
     for j in range(NY - 1):
         arrived(r3.at[j], r_3.at[j])
@@ -175,11 +195,10 @@
     d_out[...] = total[2]
 
     m_out[y] = total[:2]
+    for j in FAR_FIRST:
+        send(fin, m_out.at[y], s_f.at[j - 1], r_f.at[j - 1], here.at_y(mod(y + j, NY)))
     for j in range(1, NY):
-        to = (y + j) % NY
-        send(fin, m_out.at[y], s_f.at[j - 1], r_f.at[j - 1], device(x, to, z, c))
-    for j in range(1, NY):
-        arrived(m_out.at[(y - j + NY) % NY], r_f.at[j - 1])
+        arrived(m_out.at[mod(y - j + NY, NY)], r_f.at[j - 1])
 
     @pl.loop(0, NZ)
     def _(i):
@@ -259,8 +278,7 @@
         load.start()
     for load in loads:
         load.wait()
-    _, y, _, _ = place()
-    second = (y % 2) == 1
+    second = mod(Place().y, 2) == 1
     packed = m_ref[...].reshape(BLK, BLK)
     extra = jnp.broadcast_to(d_ref[...][None], (16, 8, BLK)).reshape(BLK, BLK)
     row = lax.broadcasted_iota(jnp.int32, (BLK, BLK), 0)
@@ -298,25 +316,41 @@
     )(packed, extra)
 
 
-def spread_kernel(inv, owner_a, owner_g, r4, rg, r5,
-                  kept, sh, sg, s_l, s_p, r_p, s_z, r_z, s_k, r_k, s_q, r_q, s_4, r_4, s_g, r_g, s_5, r_5):
-    x, y, z, c = place()
-    own = lax.axis_index("own")
-    yh, q = y // NYL, y % 2
-    sib = device(x, y, z, 1 - c)
-    beside = [device(x, (y + step) % NY, z, core) for core in (c, 1 - c) for step in (1, NY - 1)]
+def spread_kernel(inv, owner_a, owner_g, r4, r5,
+                  kept, es, er, s4, s_l, s_p, r_p, s_z, r_z, s_q, r_q, s_e, r_e, s_4, r_4, s_5, r_5):
+    here = Place()
+    x, y, z, c, yh, own = here.x, here.y, here.z, here.c, here.yh, here.own
+    q = mod(y, 2)
+    sib = here.other_core()
+    beside = [here.at_y(mod(y + step, NY)) for step in (1, NY - 1)]
 
     barrier = pltpu.get_barrier_semaphore()
     for to in [sib] + beside:
         pl.semaphore_signal(barrier, inc=1, device_id=to, device_id_type=MESH)
     for j in range(1, NX):
-        for core in (c, 1 - c):
-            pl.semaphore_signal(barrier, inc=1, device_id=device((x + j) % NX, y, z, core), device_id_type=MESH)
+        pl.semaphore_signal(barrier, inc=1, device_id=here.at_x(mod(x + j, NX)), device_id_type=MESH)
     for j in range(1, NZ):
-        pl.semaphore_signal(barrier, inc=1, device_id=device(x, y, (z + j) % NZ, c), device_id_type=MESH)
-
-    mine_here = pltpu.make_async_copy(inv.at[pl.ds(pl.multiple_of(32 * x, 32), 32)], kept.at[c, q, z, x], s_l)
+        pl.semaphore_signal(barrier, inc=1, device_id=here.at_z(mod(z + j, NZ)), device_id_type=MESH)
+
+    mine_here = pltpu.make_async_copy(inv.at[pl.ds(pl.multiple_of(32 * x, 32), 32)], kept.at[q, z, x], s_l)
     mine_here.start()
+    pl.semaphore_wait(barrier, 1 + (NX - 1) + 2 + (NZ - 1))
+    for j in (2, 1, 3):
+        to = mod(x + j, NX)
+        send(inv.at[pl.ds(pl.multiple_of(32 * to, 32), 32)], kept.at[q, z, x],
+             s_p.at[j - 1], r_p.at[j - 1], here.at_x(to))
+    mine_here.wait()
+    for j in range(1, NX):
+        arrived(kept.at[q, z, mod(x - j + NX, NX)], r_p.at[j - 1])
+    for j in FAR_FIRST:
+        send(kept.at[q, z], kept.at[q, z], s_z.at[j - 1], r_z.at[j - 1], here.at_z(mod(z + j, NZ)))
+
+    def to_neighbours(zz, j):
+        for k in range(2):
+            half = kept.at[q, zz, pl.ds(2 * k, 2)]
+            send(half, half, s_q.at[j, k], r_q.at[j, k], beside[k])
+
+    to_neighbours(z, 0)
 
     def find_a(b, found):
         at = owner_a[b] - 3 * own
@@ -330,87 +364,81 @@
     slot_g = lax.fori_loop(0, 32, find_g, zero)
 
     def at_a(b):
-        return b // 48, b % 2, (b % 48) // 6, (b % 6) // 2
+        return mod(b, 2), lax.div(mod(b, 48), 6), lax.div(mod(b, 6), 2)
 
     def at_g(b):
-        return b // 16, b % 2, (b % 16) // 2, 3
-
-    want = [at_a(jnp.where(c == 0, slot_a[k], 3 * own + k)) for k in range(3)] + [at_g(slot_g)]
-    mine_here.wait()
-    pl.semaphore_wait(barrier, 5 + 2 * (NX - 1) + (NZ - 1))
-
+        return mod(b, 2), lax.div(mod(b, 16), 2), 3
+
+    def entry(core, k):
+        if k == 3:
+            return lax.div(slot_g, 16), at_g(slot_g)
+        block = jnp.where(core == 0, slot_a[k], 3 * own + k)
+        return lax.div(block, 48), at_a(block)
+
+    mine = [entry(c, k) for k in range(4)]
+    theirs = [entry(1 - c, k) for k in range(4)]
+    for j in FAR_FIRST:
+        zz = mod(z - j + NZ, NZ)
+        arrived(kept.at[q, zz], r_z.at[j - 1])
+        to_neighbours(zz, j)
+    for j in range(NZ):
+        zz = mod(z - j + NZ, NZ)
+        for k in range(2):
+            arrived(kept.at[1 - q, zz, pl.ds(2 * k, 2)], r_q.at[j, k])
+
+    for k in range(4):
+        es[k] = kept[theirs[k][1]]
+    for m in range(2):
+        for k in range(2):
+            es[4 + 2 * m + k] = kept[at_g(8 * (2 * c + m) + 4 * yh + 2 * (1 - c) + k)]
+    send(es, er, s_e.at[0], r_e.at[0], sib)
+    values = [kept[mine[k][1]] for k in range(4)]
+    arrived(er, r_e.at[0])
+    values = [jnp.where(mine[k][0] == c, values[k], er[k]) for k in range(4)]
+    for j in range(1, NX + 1):
+        to = mod(x + j, NX)
+        for k in range(4):
+            s4[to, k] = values[k]
+        for k in range(2):
+            own_half = kept[at_g(8 * to + 4 * yh + 2 * c + k)]
+            s4[to, 4 + k] = jnp.where(lax.div(to, 2) == c, own_half, er[4 + 2 * mod(to, 2) + k])
+        if j < NX:
+            send(s4.at[to], r4.at[x], s_4.at[j - 1], r_4.at[j - 1], here.at_x(to))
+    r4[x] = s4[x]
+    send(s4.at[x, pl.ds(0, 4)], r5.at[x], s_5.at[0], r_5.at[0], sib)
     for j in range(1, NX):
-        to = (x + j) % NX
-        send(inv.at[pl.ds(pl.multiple_of(32 * to, 32), 32)], kept.at[c, q, z, x],
-             s_p.at[j - 1], r_p.at[j - 1], device(to, y, z, c))
-    for j in range(1, NX):
-        arrived(kept.at[c, q, z, (x - j + NX) % NX], r_p.at[j - 1])
-    for j in range(1, NZ):
-        send(kept.at[c, q, z], kept.at[c, q, z], s_z.at[j - 1], r_z.at[j - 1], device(x, y, (z + j) % NZ, c))
-
-    def pass_on(zz, j):
-        for k in range(4):
-            half = kept.at[c, q, zz, pl.ds(2 * (k % 2), 2)]
-            send(half, half, s_q.at[j, k], r_q.at[j, k], beside[k])
-        send(kept.at[c, q, zz], kept.at[c, q, zz], s_k.at[j], r_k.at[j], sib)
-
-    pass_on(z, 0)
-    for j in range(1, NZ):
-        zz = (z - j + NZ) % NZ
-        arrived(kept.at[c, q, zz], r_z.at[j - 1])
-        pass_on(zz, j)
+        frm = mod(x - j + NX, NX)
+        arrived(r4.at[frm], r_4.at[j - 1])
+        send(r4.at[frm, pl.ds(0, 4)], r5.at[frm], s_5.at[j], r_5.at[j], sib)
+    for j in range(NX):
+        arrived(r5.at[mod(x - j + NX, NX)], r_5.at[j])
+
     for j in range(NZ):
-        zz = (z - j + NZ) % NZ
-        arrived(kept.at[1 - c, q, zz], r_k.at[j])
-        for k in range(4):
-            arrived(kept.at[(c + k // 2) % 2, 1 - q, zz, pl.ds(2 * (k % 2), 2)], r_q.at[j, k])
-
-    for k in range(4):
-        sh[k] = kept[want[k]]
-    for j in range(1, NX + 1):
-        to = (x + j) % NX
         for k in range(2):
-            sg[to, k] = kept[at_g(8 * to + 4 * yh + 2 * c + k)]
-        if j < NX:
-            send(sh, r4.at[x], s_4.at[j - 1], r_4.at[j - 1], device(to, y, z, c))
-            send(sh, r5.at[x], s_5.at[j - 1], r_5.at[j - 1], device(to, y, z, 1 - c))
-            send(sg.at[to], rg.at[x], s_g.at[j - 1], r_g.at[j - 1], device(to, y, z, c))
-    send(sh, r5.at[x], s_5.at[NX - 1], r_5.at[NX - 1], sib)
-    r4[x] = sh[...]
-    rg[x] = sg[x]
-    for j in range(1, NX):
-        frm = (x - j + NX) % NX
-        arrived(r4.at[frm], r_4.at[j - 1])
-        arrived(rg.at[frm], r_g.at[j - 1])
-        arrived(r5.at[frm], r_5.at[j - 1])
-    arrived(r5.at[x], r_5.at[NX - 1])
-
-    for j in range(NZ):
-        for k in range(4):
-            arrived(kept.at[c, q, j, pl.ds(0, 2)], s_q.at[j, k])
-        arrived(kept.at[c, q, j], s_k.at[j])
+            arrived(kept.at[q, j, pl.ds(2 * k, 2)], s_q.at[j, k])
     for j in range(NZ - 1):
-        arrived(kept.at[c, q, z], s_z.at[j])
+        arrived(kept.at[q, z], s_z.at[j])
     for j in range(NX - 1):
-        arrived(kept.at[c, q, z, x], s_p.at[j])
-        arrived(sh, s_4.at[j])
-        arrived(sg.at[0], s_g.at[j])
+        arrived(kept.at[q, z, x], s_p.at[j])
+        arrived(s4.at[j], s_4.at[j])
+    arrived(es, s_e.at[0])
     for j in range(NX):
-        arrived(sh, s_5.at[j])
+        arrived(r5.at[j], s_5.at[j])
 
 
 def spread(inv, owner_a, owner_g):
     dma = pltpu.SemaphoreType.DMA
     vm = pltpu.VMEM
     piece = (32, BLK)
-    shapes = ((NX - 1,), (NZ - 1,), (NZ,), (NZ, 4), (NX - 1,), (NX - 1,), (NX,))
+    shapes = ((NX - 1,), (NZ - 1,), (NZ, 2), (1,), (NX - 1,), (NX,))
     return pl.pallas_call(
         spread_kernel,
-        out_shape=tuple(jax.ShapeDtypeStruct((NX, n) + piece, BF16) for n in (4, 2, 4)),
+        out_shape=(jax.ShapeDtypeStruct((NX, 6) + piece, BF16), jax.ShapeDtypeStruct((NX, 4) + piece, BF16)),
         in_specs=[pl.BlockSpec(memory_space=pl.ANY)] + [pl.BlockSpec(memory_space=pltpu.SMEM)] * 2,
-        out_specs=[pl.BlockSpec(memory_space=pltpu.VMEM)] * 3,
-        scratch_shapes=[vm((2, 2, NZ, NX) + piece, BF16), vm((4,) + piece, BF16), vm((NX, 2) + piece, BF16), dma]
-        + [dma(shape) for shape in shapes for _ in range(2)],
+        out_specs=[pl.BlockSpec(memory_space=pltpu.VMEM)] * 2,
+        scratch_shapes=[
+            vm((2, NZ, NX) + piece, BF16), vm((8,) + piece, BF16), vm((8,) + piece, BF16), vm((NX, 6) + piece, BF16), dma,
+        ] + [dma(shape) for shape in shapes for _ in range(2)],
         compiler_params=pltpu.CompilerParams(
             collective_id=1, has_side_effects=True, vmem_limit_bytes=62 * 2**20
         ),
@@ -418,11 +446,11 @@
     )(inv, owner_a, owner_g)
 
 
-def apply_kernel(r4_hbm, rg_hbm, r5_hbm, w_hbm, a_hbm, g_hbm, p_hbm, r4, rg, r5, w, a_out, g_out, p_out, s_in, s_out):
-    _, _, _, c = place()
+def apply_kernel(r4_hbm, r5_hbm, w_hbm, a_hbm, g_hbm, p_hbm, r4, r5, w, a_out, g_out, p_out, s_in, s_out):
+    c = Place().c
     loads = [
         pltpu.make_async_copy(src, dst, s_in.at[k])
-        for k, (src, dst) in enumerate(((r4_hbm, r4), (rg_hbm, rg), (r5_hbm, r5), (w_hbm, w)))
+        for k, (src, dst) in enumerate(((r4_hbm, r4), (r5_hbm, r5), (w_hbm, w)))
     ]
     for load in loads:
         load.start()
@@ -432,8 +460,7 @@
     def whole(ref, k):
         return ref[:, k].reshape(BLK, BLK)
 
-    mine = [whole(r4, k) for k in range(4)]
-    right = [whole(rg, k) for k in range(2)]
+    mine = [whole(r4, k) for k in range(6)]
     theirs = [whole(r5, k) for k in range(4)]
     core0 = c == 0
     stores = []
@@ -448,7 +475,7 @@
         left = jnp.dot(placed, w[rows, :], preferred_element_type=F32).astype(BF16)
         for m in range(2):
             cols = slice(BLK * m, BLK * (m + 1))
-            p_out[rows, cols] = jnp.dot(left[:, cols], right[m], preferred_element_type=F32)
+            p_out[rows, cols] = jnp.dot(left[:, cols], mine[4 + m], preferred_element_type=F32)
         store(p_out.at[rows], p_hbm.at[rows])
     for k in range(3):
         a_out[k] = jnp.where(core0, mine[k], theirs[k])
@@ -459,7 +486,7 @@
         each.wait()
 
 
-def apply_inverses(r4, rg, r5, w):
+def apply_inverses(r4, r5, w):
     outs = (
         jax.ShapeDtypeStruct((3, BLK, BLK), BF16),
         jax.ShapeDtypeStruct((1, BLK, BLK), BF16),
@@ -468,13 +495,13 @@
     return pl.pallas_call(
         apply_kernel,
         out_shape=outs,
-        in_specs=[pl.BlockSpec(memory_space=pl.ANY)] * 4,
+        in_specs=[pl.BlockSpec(memory_space=pl.ANY)] * 3,
         out_specs=[pl.BlockSpec(memory_space=pl.ANY)] * 3,
-        scratch_shapes=[pltpu.VMEM(a.shape, a.dtype) for a in (r4, rg, r5, w) + outs]
-        + [pltpu.SemaphoreType.DMA((4,)), pltpu.SemaphoreType.DMA((5,))],
+        scratch_shapes=[pltpu.VMEM(a.shape, a.dtype) for a in (r4, r5, w) + outs]
+        + [pltpu.SemaphoreType.DMA((3,)), pltpu.SemaphoreType.DMA((5,))],
         compiler_params=pltpu.CompilerParams(vmem_limit_bytes=62 * 2**20),
         name="apply_inverses",
-    )(r4, rg, r5, w)
+    )(r4, r5, w)
 
 
 def on_device(hidden_act, out_grad, weight_grad, owner_a, owner_g):

time: 88.6 us -> 84.4 us (0.953)
  Pallas kernels: 87.7 us -> 83.5 us
    pallas_call x1, Pallas kernels: 30.5 us -> 28 us  [spread(): pl.pallas_call(spread_kernel, out_shape=(jax.ShapeDtypeStruct((NX, 6) + p...]
    pallas_call x1, Pallas kernels: 50.6 us -> 48.9 us  [gram_sums(): pl.pallas_call(gram_kernel, out_shape=(jax.ShapeDtypeStruct((NY, 2) + til...]
where the time goes in v4:
time: 84.4 us; the launch traced here: 84.2 us
  Pallas kernels  83.5 us (99%)
    pallas_call x1, Pallas kernels, gram_sums(): pl.pallas_call(gram_kernel, out_shape=(jax.ShapeDtypeStruct((NY, 2) + til...  48.9 us
    pallas_call x1, Pallas kernels, spread(): pl.pallas_call(spread_kernel, out_shape=(jax.ShapeDtypeStruct((NX, 6) + p...  28 us
    pallas_call x1, Pallas kernels, newton(): pl.pallas_call(lambda *refs: newton_kernel(token_total, *refs), out_shape...  4.39 us
    pallas_call x1, Pallas kernels, apply_inverses(): pl.pallas_call(apply_kernel, out_shape=outs, in_specs=[pl.BlockSpec(memor...  2.23 us

profile of v4, /device:TPU:1, one launch (start us, length us, event | category | flops | bytes accessed | tf_op | source)
XLA Modules:
  0.0 84.2 jit_solution(14511449509814944363)
XLA Ops:
  0.6 48.9 %gram_sums.1 = (f32[8,2,8,128]{3,2,1,0:T(8,128)}, f32[8,128]{1,0:T(8,128)}) custom-call(bf16[128,12288]{1,0:T(8,128)(2,1)} %hid.1, bf16[128,4096]{1,0:T(8,128)(2,1)} %grd.1), custom_call_target="tpu_custom_call" | custom-call | flops 536870912 | bytes 4194304 | tf_op jit(solution)/shard_map/gram_sums/pallas_call | solution.py:227
  49.5 4.4 %newton.1.inv = bf16[128,128]{1,0:T(8,128)(2,1)} custom-call(f32[8,2,8,128]{3,2,1,0:T(8,128)} %get-tuple-element.7.refs_0_, f32[8,128]{1,0:T(8,128)} %get-tuple-element.8.refs_1_), custom_call_target="tpu_custom_call" | custom-call | tf_op jit(solution)/shard_map/newton/pallas_call | solution.py:308
  53.9 28.0 %spread_inverses.1 = (bf16[4,6,32,128]{3,2,1,0:T(8,128)(2,1)}, bf16[4,4,32,128]{3,2,1,0:T(8,128)(2,1)}) custom-call(bf16[128,128]{1,0:T(8,128)(2,1)} %newton.1.inv, s32[96]{0:T(128)} %owner_a.1, s32[32]{0:T(128)} %owner_g.1), custom_call_target="tpu_custom_call" | custom-call | tf_op jit(solution)/shard_map/spread_inverses/pallas_call | solution.py:434
  81.9 2.2 %apply_inverses.1 = (bf16[3,128,128]{2,1,0:T(8,128)(2,1)}, bf16[1,128,128]{2,1,0:T(8,128)(2,1)}, f32[384,256]{1,0:T(8,128)}) custom-call(bf16[4,6,32,128]{3,2,1,0:T(8,128)(2,1)} %get-tuple-element.9.r4_hbm, bf16[4,4,32,128]{3,2,1,0:T(8,128)(2,1)} %get-tuple-element.10.r5_hbm, bf16[384,256]{1,0:T(8,128)(2,1)} %w_hbm.1), custom_call_target="tpu_custom_call" | custom-call | tf_op jit(solution)/shard_map/apply_inverses/pallas_call | solution.py:495

commit v5 on v4

--- a/solution.py
+++ b/solution.py
@@ -56,7 +56,7 @@
 
 
 def gram_kernel(hid, grd, m_out, d_out,
-                raw, ta, tg, ra, rz, rg, rx, a3, r3, fin,
+                raw, ta, tg, ru, rv, rw, rz, rg, rx, a3, r3, fin,
                 s_loc, s_raw_s, s_raw_r, s_a, r_a, s_z, r_z, s_g, r_g, s_x, r_x, s_3, r_3, s_f, r_f):
     here = Place()
     x, y, z, c = here.x, here.y, here.z, here.c
@@ -76,6 +76,10 @@
 
     def onward(i):
         return here.at_z(mod(z + NZ + 1 - 2 * mod(i, 2), NZ))
+
+    def x_ways(i):
+        turn = 2 * mod(i, 2)
+        return mod(x + 1 + turn, NX), mod(x + 3 - turn, NX)
 
     def parts(zz, core, rows):
         return (
@@ -123,9 +127,9 @@
             ta[zz, xx, pl.ds(0, NY)] = packed[:, 0]
             ta[zz, xx, NY] = extra
             tg[zz, xx] = packed[:, 1]
-        for j in (2, 1, 3):
-            to = mod(x + j, NX)
-            send(ta.at[zz, to], ra.at[j - 1, zz], s_a.at[j - 1, i], r_a.at[j - 1, i], here.at_x(to))
+        ahead, back = x_ways(i)
+        send(ta.at[zz, mod(x + 2, NX)], ru.at[i], s_a.at[0, i], r_a.at[0, i], here.at_x(ahead))
+        send(ta.at[zz, back], rv.at[i], s_a.at[1, i], r_a.at[1, i], here.at_x(back))
         for xx in range(NX):
             if not first:
                 arrived(rg.at[i - 2, xx], r_g.at[i - 2, xx])
@@ -137,12 +141,18 @@
             if not last:
                 send(tg.at[zz, xx], rg.at[i, xx], s_g.at[i, xx], r_g.at[i, xx], onward(i))
 
+    def x_step(i):
+        zz = target(i)
+        ahead, _ = x_ways(i)
+        arrived(ru.at[i], r_a.at[0, i])
+        ta[zz, ahead] = ta[zz, ahead] + ru[i]
+        send(ta.at[zz, ahead], rw.at[i], s_a.at[2, i], r_a.at[2, i], here.at_x(ahead))
+
     def tile0_step(i, first, last):
         zz = target(i)
-        total = ta[zz, x]
-        for j in range(NX - 1):
-            arrived(ra.at[j, zz], r_a.at[j, i])
-            total = total + ra[j, zz]
+        arrived(rv.at[i], r_a.at[1, i])
+        arrived(rw.at[i], r_a.at[2, i])
+        total = ta[zz, x] + rv[i] + rw[i]
         if not first:
             arrived(rz.at[i - 2], r_z.at[i - 2])
             total = total + rz[i - 2]
@@ -158,21 +168,30 @@
     def _(i):
         gram_step(i, True, False)
 
-    @pl.loop(2, 4)
+    gram_step(2, False, False)
+    x_step(0)
+    x_step(1)
+
+    @pl.loop(3, 5)
     def _(i):
         gram_step(i, False, False)
-        tile0_step(i - 2, True, False)
-
-    @pl.loop(4, 7)
+        x_step(i - 1)
+        tile0_step(i - 3, True, False)
+
+    @pl.loop(5, 7)
     def _(i):
         gram_step(i, False, False)
-        tile0_step(i - 2, False, False)
+        x_step(i - 1)
+        tile0_step(i - 3, False, False)
 
     gram_step(7, False, True)
     for j in (2, 1, 3):
         to = mod(x + j, NX)
         send(tg.at[z, to], rx.at[j - 1], s_x.at[j - 1], r_x.at[j - 1], here.at_x(to))
+    x_step(6)
+    tile0_step(4, False, False)
     tile0_step(5, False, False)
+    x_step(7)
     tile0_step(6, False, False)
     total0 = tile0_step(7, False, True)
     total1 = tg[z, x]
@@ -233,7 +252,9 @@
             vm((256, 8192), BF16),
             vm((NZ, NX, NY + 1) + tile, F32),
             vm((NZ, NX, NY) + tile, F32),
-            vm((NX - 1, NZ, NY + 1) + tile, F32),
+            vm((NZ, NY + 1) + tile, F32),
+            vm((NZ, NY + 1) + tile, F32),
+            vm((NZ, NY + 1) + tile, F32),
             vm((NZ - 1, NY + 1) + tile, F32),
             vm((NZ - 1, NX, NY) + tile, F32),
             vm((NX - 1, NY) + tile, F32),
@@ -325,16 +346,15 @@
     beside = [here.at_y(mod(y + step, NY)) for step in (1, NY - 1)]
 
     barrier = pltpu.get_barrier_semaphore()
-    for to in [sib] + beside:
+    onward, back = here.at_z(mod(z + 1, NZ)), here.at_z(mod(z + NZ - 1, NZ))
+    for to in [sib, onward, back] + beside:
         pl.semaphore_signal(barrier, inc=1, device_id=to, device_id_type=MESH)
     for j in range(1, NX):
         pl.semaphore_signal(barrier, inc=1, device_id=here.at_x(mod(x + j, NX)), device_id_type=MESH)
-    for j in range(1, NZ):
-        pl.semaphore_signal(barrier, inc=1, device_id=here.at_z(mod(z + j, NZ)), device_id_type=MESH)
 
     mine_here = pltpu.make_async_copy(inv.at[pl.ds(pl.multiple_of(32 * x, 32), 32)], kept.at[q, z, x], s_l)
     mine_here.start()
-    pl.semaphore_wait(barrier, 1 + (NX - 1) + 2 + (NZ - 1))
+    pl.semaphore_wait(barrier, 1 + (NX - 1) + 2 + 2)
     for j in (2, 1, 3):
         to = mod(x + j, NX)
         send(inv.at[pl.ds(pl.multiple_of(32 * to, 32), 32)], kept.at[q, z, x],
@@ -342,8 +362,12 @@
     mine_here.wait()
     for j in range(1, NX):
         arrived(kept.at[q, z, mod(x - j + NX, NX)], r_p.at[j - 1])
-    for j in FAR_FIRST:
-        send(kept.at[q, z], kept.at[q, z], s_z.at[j - 1], r_z.at[j - 1], here.at_z(mod(z + j, NZ)))
+
+    def along_z(zz, k, to):
+        send(kept.at[q, zz], kept.at[q, zz], s_z.at[k], r_z.at[k], to)
+
+    along_z(z, 0, onward)
+    along_z(z, 4, back)
 
     def to_neighbours(zz, j):
         for k in range(2):
@@ -377,10 +401,18 @@
 
     mine = [entry(c, k) for k in range(4)]
     theirs = [entry(1 - c, k) for k in range(4)]
-    for j in FAR_FIRST:
+    for j in range(1, 5):
         zz = mod(z - j + NZ, NZ)
         arrived(kept.at[q, zz], r_z.at[j - 1])
+        if j < 4:
+            along_z(zz, j, onward)
         to_neighbours(zz, j)
+        if j < 4:
+            zz = mod(z + j, NZ)
+            arrived(kept.at[q, zz], r_z.at[3 + j])
+            if j < 3:
+                along_z(zz, 4 + j, back)
+            to_neighbours(zz, NZ - j)
     for j in range(NZ):
         zz = mod(z - j + NZ, NZ)
         for k in range(2):

time: 84.4 us -> 91.8 us (1.088)
  Pallas kernels: 83.5 us -> 91 us
    pallas_call x1, Pallas kernels: 28 us -> 33.8 us  [spread(): pl.pallas_call(spread_kernel, out_shape=(jax.ShapeDtypeStruct((NX, 6) + p...]
    pallas_call x1, Pallas kernels: 48.9 us -> 50.5 us  [gram_sums(): pl.pallas_call(gram_kernel, out_shape=(jax.ShapeDtypeStruct((NY, 2) + til...]
where the time goes in v5:
time: 91.8 us; the launch traced here: 91.6 us
  Pallas kernels  91 us (99%)
    pallas_call x1, Pallas kernels, gram_sums(): pl.pallas_call(gram_kernel, out_shape=(jax.ShapeDtypeStruct((NY, 2) + til...  50.5 us
    pallas_call x1, Pallas kernels, spread(): pl.pallas_call(spread_kernel, out_shape=(jax.ShapeDtypeStruct((NX, 6) + p...  33.8 us
    pallas_call x1, Pallas kernels, newton(): pl.pallas_call(lambda *refs: newton_kernel(token_total, *refs), out_shape...  4.39 us
    pallas_call x1, Pallas kernels, apply_inverses(): pl.pallas_call(apply_kernel, out_shape=outs, in_specs=[pl.BlockSpec(memor...  2.23 us

profile of v5, /device:TPU:1, one launch (start us, length us, event | category | flops | bytes accessed | tf_op | source)
XLA Modules:
  0.0 91.6 jit_solution(7304989550695805024)
XLA Ops:
  0.6 50.5 %gram_sums.1 = (f32[8,2,8,128]{3,2,1,0:T(8,128)}, f32[8,128]{1,0:T(8,128)}) custom-call(bf16[128,12288]{1,0:T(8,128)(2,1)} %hid.1, bf16[128,4096]{1,0:T(8,128)(2,1)} %grd.1), custom_call_target="tpu_custom_call" | custom-call | flops 536870912 | bytes 4194304 | tf_op jit(solution)/shard_map/gram_sums/pallas_call | solution.py:246
  51.2 4.4 %newton.1.inv = bf16[128,128]{1,0:T(8,128)(2,1)} custom-call(f32[8,2,8,128]{3,2,1,0:T(8,128)} %get-tuple-element.7.refs_0_, f32[8,128]{1,0:T(8,128)} %get-tuple-element.8.refs_1_), custom_call_target="tpu_custom_call" | custom-call | tf_op jit(solution)/shard_map/newton/pallas_call | solution.py:329
  55.5 33.8 %spread_inverses.1 = (bf16[4,6,32,128]{3,2,1,0:T(8,128)(2,1)}, bf16[4,4,32,128]{3,2,1,0:T(8,128)(2,1)}) custom-call(bf16[128,128]{1,0:T(8,128)(2,1)} %newton.1.inv, s32[96]{0:T(128)} %owner_a.1, s32[32]{0:T(128)} %owner_g.1), custom_call_target="tpu_custom_call" | custom-call | tf_op jit(solution)/shard_map/spread_inverses/pallas_call | solution.py:466
  89.4 2.2 %apply_inverses.1 = (bf16[3,128,128]{2,1,0:T(8,128)(2,1)}, bf16[1,128,128]{2,1,0:T(8,128)(2,1)}, f32[384,256]{1,0:T(8,128)}) custom-call(bf16[4,6,32,128]{3,2,1,0:T(8,128)(2,1)} %get-tuple-element.9.r4_hbm, bf16[4,4,32,128]{3,2,1,0:T(8,128)(2,1)} %get-tuple-element.10.r5_hbm, bf16[384,256]{1,0:T(8,128)(2,1)} %w_hbm.1), custom_call_target="tpu_custom_call" | custom-call | tf_op jit(solution)/shard_map/apply_inverses/pallas_call | solution.py:527

commit v6 on v2

--- a/solution.py
+++ b/solution.py
@@ -7,6 +7,7 @@
 
 BLK = 128
 ITERS = 14
+FINE = 4
 DAMPING = 0.05
 NX, NY, NZ, NYL = 4, 8, 8, 4
 MESH = pl.DeviceIdType.MESH
@@ -14,14 +15,32 @@
 BF16 = jnp.bfloat16
 
 
-def place():
-    dp = lax.axis_index("dp")
-    own = lax.axis_index("own")
-    return dp // 4, ((dp // 2) % 2) * NYL + own % NYL, own // NYL, dp % 2
-
-
-def device(x, y, z, c):
-    return (x * 4 + (y // NYL) * 2 + c, z * NYL + y % NYL)
+FAR_FIRST = (4, 3, 5, 2, 6, 1, 7)
+
+
+def mod(value, n):
+    return value % n if isinstance(value, int) else lax.rem(value, n)
+
+
+class Place:
+    def __init__(self):
+        self.dp, self.own = lax.axis_index("dp"), lax.axis_index("own")
+        self.x, self.c = lax.div(self.dp, 4), mod(self.dp, 2)
+        self.yh = mod(lax.div(self.dp, 2), 2)
+        self.z, self.yl = lax.div(self.own, NYL), mod(self.own, NYL)
+        self.y = self.yh * NYL + self.yl
+
+    def at_x(self, to):
+        return (self.dp + 4 * (to - self.x), self.own)
+
+    def at_y(self, to):
+        return (self.dp + 2 * (lax.div(to, NYL) - self.yh), self.own + mod(to, NYL) - self.yl)
+
+    def at_z(self, to):
+        return (self.dp, self.own + NYL * (to - self.z))
+
+    def other_core(self):
+        return (self.dp + 1 - 2 * self.c, self.own)
 
 
 def send(src, dst, send_sem, recv_sem, to):
@@ -40,41 +59,32 @@
                 raw, ta, tb, tg, ra, rb, rg, a2, b2, g2, ra2, rb2, rg2, a3, x3, ra3, rx3, fin,
                 s_loc, s_raw_s, s_raw_r, s_a, r_a, s_b, r_b, s_g, r_g,
                 s_a2, r_a2, s_b2, r_b2, s_g2, r_g2, s_a3, r_a3, s_x3, r_x3, s_f, r_f):
-    x, y, z, c = place()
-    sib = device(x, y, z, 1 - c)
+    here = Place()
+    x, y, z, c = here.x, here.y, here.z, here.c
+    sib = here.other_core()
 
     barrier = pltpu.get_barrier_semaphore()
     pl.semaphore_signal(barrier, inc=1, device_id=sib, device_id_type=MESH)
     for j in range(1, NX):
-        pl.semaphore_signal(barrier, inc=1, device_id=device((x + j) % NX, y, z, c), device_id_type=MESH)
+        pl.semaphore_signal(barrier, inc=1, device_id=here.at_x(mod(x + j, NX)), device_id_type=MESH)
     for j in range(1, NY):
-        pl.semaphore_signal(barrier, inc=1, device_id=device(x, (y + j) % NY, z, c), device_id_type=MESH)
+        pl.semaphore_signal(barrier, inc=1, device_id=here.at_y(mod(y + j, NY)), device_id_type=MESH)
     for j in range(1, NZ):
-        pl.semaphore_signal(barrier, inc=1, device_id=device(x, y, (z + j) % NZ, c), device_id_type=MESH)
-
-    def local_parts(zz, core, rows):
+        pl.semaphore_signal(barrier, inc=1, device_id=here.at_z(mod(z + j, NZ)), device_id_type=MESH)
+
+    def halves(core, rows):
         return (
-            (hid.at[:, pl.ds(pl.multiple_of(6144 * core + 768 * zz, 128), 768)],
-             raw.at[rows, pl.ds(pl.multiple_of(1024 * zz, 128), 768)]),
-            (grd.at[:, pl.ds(pl.multiple_of(2048 * core + 256 * zz, 128), 256)],
-             raw.at[rows, pl.ds(pl.multiple_of(1024 * zz + 768, 128), 256)]),
+            (hid.at[:, pl.ds(pl.multiple_of(6144 * core, 128), 6144)], raw.at[rows, pl.ds(0, 6144)]),
+            (grd.at[:, pl.ds(pl.multiple_of(2048 * core, 128), 2048)], raw.at[rows, pl.ds(6144, 2048)]),
         )
 
     low, high = pl.ds(0, 128), pl.ds(128, 128)
-
-    @pl.loop(0, NZ)
-    def _(i):
-        zz = (z + 1 + i) % NZ
-        for k, (src, dst) in enumerate(local_parts(zz, c, low)):
-            pltpu.make_async_copy(src, dst, s_loc.at[i, k]).start()
-
+    own_part = [pltpu.make_async_copy(src, dst, s_loc.at[k]) for k, (src, dst) in enumerate(halves(c, low))]
+    for part in own_part:
+        part.start()
     pl.semaphore_wait(barrier, 1 + (NX - 1) + (NY - 1) + (NZ - 1))
-
-    @pl.loop(0, NZ)
-    def _(i):
-        zz = (z + 1 + i) % NZ
-        for k, (src, dst) in enumerate(local_parts(zz, 1 - c, high)):
-            send(src, dst, s_raw_s.at[i, k], s_raw_r.at[i, k], sib)
+    for k, (src, dst) in enumerate(halves(1 - c, high)):
+        send(src, dst, s_raw_s.at[k], s_raw_r.at[k], sib)
 
     row8 = lax.broadcasted_iota(jnp.int32, (BLK, BLK), 0) // 8
     col8 = lax.broadcasted_iota(jnp.int32, (BLK, BLK), 1) // 8
@@ -82,56 +92,66 @@
     middle = row8 == col8
 
     def gram(zz, k):
-        cols = pl.ds(pl.multiple_of(1024 * zz + BLK * k, BLK), BLK)
+        at = 768 * zz + BLK * k if k < 6 else 6144 + 256 * zz + BLK * (k - 6)
+        cols = pl.ds(pl.multiple_of(at, BLK), BLK)
         tok = raw[:, cols]
         return lax.dot_general(tok, tok, (((0,), (0,)), ((), ())), preferred_element_type=F32)
 
-    @pl.loop(0, NZ)
-    def _(i):
-        zz = (z + 1 + i) % NZ
-        for k, (src, dst) in enumerate(local_parts(zz, c, low)):
-            pltpu.make_async_copy(src, dst, s_loc.at[i, k]).wait()
-        for k, (src, dst) in enumerate(local_parts(zz, c, high)):
-            arrived(dst, s_raw_r.at[i, k])
+    for part in own_part:
+        part.wait()
+    for k, (src, dst) in enumerate(halves(c, high)):
+        arrived(dst, s_raw_r.at[k])
+
+    def gram_step(i):
+        zz = mod(z + 1 + i, NZ)
         for xx in range(NX):
             first = gram(zz, 2 * xx)
             second = gram(zz, 2 * xx + 1)
             packed = jnp.where(upper, first, second).reshape(NY, 2, 8, BLK)
             extra = jnp.sum(jnp.where(middle, second, 0.0).reshape(16, 8, BLK), axis=0)
-            ta[zz, xx, pl.ds(0, NY)] = packed[:, 0]
-            ta[zz, xx, NY] = extra
+            ta[xx, i, pl.ds(0, NY)] = packed[:, 0]
+            ta[xx, i, NY] = extra
             if xx < 2:
                 tb[:, i, xx] = packed[:, 1]
             else:
                 tg[zz, xx - 2] = packed[:, 1]
-        for j in range(1, NX):
-            to = (x + j) % NX
-            send(ta.at[zz, to], ra.at[j - 1, zz], s_a.at[j - 1, i], r_a.at[j - 1, i], device(to, y, z, c))
-
-        @pl.when(i < NZ - 1)
+        return zz
+
+    @pl.loop(0, 4)
+    def _(k):
+        zz = gram_step(2 * k)
+        send(tg.at[zz], rg.at[2 * k], s_g.at[2 * k], r_g.at[2 * k], here.at_z(zz))
+        zz = gram_step(2 * k + 1)
+        for j in (2, 1, 3):
+            to = mod(x + j, NX)
+            send(ta.at[to, pl.ds(2 * k, 2)], ra.at[j - 1, pl.ds(2 * k, 2)], s_a.at[j - 1, k], r_a.at[j - 1, k], here.at_x(to))
+
+        @pl.when(k < 3)
         def _():
-            send(tg.at[zz], rg.at[i], s_g.at[i], r_g.at[i], device(x, y, zz, c))
-
-        @pl.when(i % 4 == 3)
+            send(tg.at[zz], rg.at[2 * k + 1], s_g.at[2 * k + 1], r_g.at[2 * k + 1], here.at_z(zz))
+
+        @pl.when(k % 2 == 1)
         def _():
-            half = i // 4
-            for j in range(1, NY):
-                to = (y + j) % NY
+            half = k // 2
+            for j in FAR_FIRST:
+                to = mod(y + j, NY)
                 send(tb.at[to, pl.ds(4 * half, 4)], rb.at[j - 1, pl.ds(4 * half, 4)],
-                     s_b.at[j - 1, half], r_b.at[j - 1, half], device(x, to, z, c))
-
-    @pl.loop(0, NZ)
-    def _(i):
-        zz = (z + 1 + i) % NZ
-        total = ta[zz, x]
+                     s_b.at[j - 1, half], r_b.at[j - 1, half], here.at_y(to))
+
+    @pl.loop(0, 4)
+    def _(k):
         for j in range(NX - 1):
-            arrived(ra.at[j, zz], r_a.at[j, i])
-            total = total + ra[j, zz]
-        a2[zz] = total
-
-        @pl.when(i < NZ - 1)
-        def _():
-            send(a2.at[zz], ra2.at[i], s_a2.at[i], r_a2.at[i], device(x, y, zz, c))
+            arrived(ra.at[j, pl.ds(2 * k, 2)], r_a.at[j, k])
+        for i in (2 * k, 2 * k + 1):
+            zz = mod(z + 1 + i, NZ)
+            total = ta[x, i]
+            for j in range(NX - 1):
+                total = total + ra[j, i]
+            a2[zz] = total
+
+            @pl.when(i < NZ - 1)
+            def _():
+                send(a2.at[zz], ra2.at[i], s_a2.at[i], r_a2.at[i], here.at_z(zz))
 
     for j in range(NZ - 1):
         arrived(rg.at[j], r_g.at[j])
@@ -141,9 +161,9 @@
             total = total + rg[j, k]
         for yy in range(NY):
             g2[yy, k] = total[yy]
-    for j in range(1, NY):
-        to = (y + j) % NY
-        send(g2.at[to], rg2.at[j - 1], s_g2.at[j - 1], r_g2.at[j - 1], device(x, to, z, c))
+    for j in FAR_FIRST:
+        to = mod(y + j, NY)
+        send(g2.at[to], rg2.at[j - 1], s_g2.at[j - 1], r_g2.at[j - 1], here.at_y(to))
 
     for j in range(NY - 1):
         for half in range(2):
@@ -155,11 +175,11 @@
         for j in range(NY - 1):
             total = total + rb[j, i]
         b2[i] = total
-        zz = (z + 1 + i) % NZ
+        zz = mod(z + 1 + i, NZ)
 
         @pl.when(i < NZ - 1)
         def _():
-            send(b2.at[i], rb2.at[i], s_b2.at[i], r_b2.at[i], device(x, y, zz, c))
+            send(b2.at[i], rb2.at[i], s_b2.at[i], r_b2.at[i], here.at_z(zz))
 
     total = a2[z]
     for j in range(NZ - 1):
@@ -168,9 +188,9 @@
     for yy in range(NY):
         a3[yy, 0] = total[yy]
         a3[yy, 1] = total[NY]
-    for j in range(1, NY):
-        to = (y + j) % NY
-        send(a3.at[to], ra3.at[j - 1], s_a3.at[j - 1], r_a3.at[j - 1], device(x, to, z, c))
+    for j in FAR_FIRST:
+        to = mod(y + j, NY)
+        send(a3.at[to], ra3.at[j - 1], s_a3.at[j - 1], r_a3.at[j - 1], here.at_y(to))
 
     total = g2[y]
     for j in range(NY - 1):
@@ -184,9 +204,9 @@
         total = total + rb2[j]
     x3[0] = total[0]
     x3[1] = total[1]
-    for j in range(1, NX):
-        to = (x + j) % NX
-        send(x3.at[to], rx3.at[j - 1], s_x3.at[j - 1], r_x3.at[j - 1], device(to, y, z, c))
+    for j in (2, 1, 3):
+        to = mod(x + j, NX)
+        send(x3.at[to], rx3.at[j - 1], s_x3.at[j - 1], r_x3.at[j - 1], here.at_x(to))
 
     total = a3[y]
     for j in range(NY - 1):
@@ -201,20 +221,17 @@
     fin[1] = total
 
     m_out[y] = fin[...]
+    for j in FAR_FIRST:
+        to = mod(y + j, NY)
+        send(fin, m_out.at[y], s_f.at[j - 1], r_f.at[j - 1], here.at_y(to))
     for j in range(1, NY):
-        to = (y + j) % NY
-        send(fin, m_out.at[y], s_f.at[j - 1], r_f.at[j - 1], device(x, to, z, c))
-    for j in range(1, NY):
-        arrived(m_out.at[(y - j + NY) % NY], r_f.at[j - 1])
-
-    @pl.loop(0, NZ)
-    def _(i):
-        zz = (z + 1 + i) % NZ
-        for k, (src, dst) in enumerate(local_parts(zz, 1 - c, high)):
-            arrived(src, s_raw_s.at[i, k])
-        for j in range(NX - 1):
-            arrived(ta.at[zz, x], s_a.at[j, i])
-
+        arrived(m_out.at[mod(y - j + NY, NY)], r_f.at[j - 1])
+
+    for k, (src, dst) in enumerate(halves(1 - c, high)):
+        arrived(src, s_raw_s.at[k])
+    for j in range(NX - 1):
+        for k in range(4):
+            arrived(ta.at[0, pl.ds(2 * k, 2)], s_a.at[j, k])
     for j in range(NZ - 1):
         arrived(tg.at[j], s_g.at[j])
         arrived(a2.at[j], s_a2.at[j])
@@ -240,7 +257,7 @@
         out_specs=[pl.BlockSpec(memory_space=pltpu.VMEM)] * 2,
         scratch_shapes=[
             vm((256, 8192), BF16),
-            vm((NZ, NX, NY + 1) + tile, F32),
+            vm((NX, NZ, NY + 1) + tile, F32),
             vm((NY, NZ, 2) + tile, F32),
             vm((NZ, 2, NY) + tile, F32),
             vm((NX - 1, NZ, NY + 1) + tile, F32),
@@ -257,8 +274,8 @@
             vm((NY - 1, 2) + tile, F32),
             vm((NX - 1,) + tile, F32),
             vm((2,) + tile, F32),
-            dma((NZ, 2)), dma((NZ, 2)), dma((NZ, 2)),
-            dma((NX - 1, NZ)), dma((NX - 1, NZ)),
+            dma((2,)), dma((2,)), dma((2,)),
+            dma((NX - 1, 4)), dma((NX - 1, 4)),
             dma((NY - 1, 2)), dma((NY - 1, 2)),
             dma((NZ - 1,)), dma((NZ - 1,)),
             dma((NZ - 1,)), dma((NZ - 1,)),
@@ -283,13 +300,15 @@
     return high, mid, (rest - mid.astype(F32)).astype(BF16)
 
 
-def product(left, right):
+def product(left, right, fine):
     lh, lm, ll = split3(left)
     rh, rm, rl = split3(right)
 
     def dot(a, b):
         return jnp.dot(a, b, preferred_element_type=F32)
 
+    if not fine:
+        return dot(jnp.concatenate((lh, lm), axis=1), jnp.concatenate((rh, rh), axis=0)) + dot(lh, rm)
     small = dot(jnp.concatenate((lm, ll), axis=1), jnp.concatenate((rm, rh), axis=0))
     middle = dot(jnp.concatenate((lh, lm), axis=1), jnp.concatenate((rm, rh), axis=0))
     large = dot(jnp.concatenate((lh, lh), axis=1), jnp.concatenate((rh, rl), axis=0))
@@ -302,8 +321,7 @@
         load.start()
     for load in loads:
         load.wait()
-    _, y, _, _ = place()
-    second = (y % 2) == 1
+    second = mod(Place().y, 2) == 1
     packed = m_ref[...].reshape(BLK, BLK)
     extra = jnp.broadcast_to(d_ref[...][None], (16, 8, BLK)).reshape(BLK, BLK)
     row = lax.broadcasted_iota(jnp.int32, (BLK, BLK), 0)
@@ -317,10 +335,11 @@
     bound = jnp.max(jnp.sum(jnp.abs(factor), axis=1, keepdims=True), axis=0, keepdims=True)
     both = jnp.concatenate((factor / bound, identity / bound), axis=1)
 
-    def refine(step, both):
-        return 2.0 * both - product(both[:, :BLK], both)
-
-    both = lax.fori_loop(0, ITERS, refine, both)
+    def refine(fine):
+        return lambda step, both: 2.0 * both - product(both[:, :BLK], both, fine)
+
+    both = lax.fori_loop(0, FINE, refine(True), both)
+    both = lax.fori_loop(FINE, ITERS, refine(False), both)
     x_ref[...] = both[:, BLK:].astype(BF16)
     store = pltpu.make_async_copy(x_ref, x_hbm, sem.at[0])
     store.start()
@@ -342,22 +361,39 @@
 
 def spread_kernel(inv, owner_a, owner_g, r4, r5,
                   kept, es, er, s4, s_l, s_p, r_p, s_z, r_z, s_q, r_q, s_e, r_e, s_4, r_4, s_5, r_5):
-    x, y, z, c = place()
-    own = lax.axis_index("own")
-    yh, q = y // NYL, y % 2
-    sib = device(x, y, z, 1 - c)
+    here = Place()
+    x, y, z, c, yh, own = here.x, here.y, here.z, here.c, here.yh, here.own
+    q = mod(y, 2)
+    sib = here.other_core()
+    beside = [here.at_y(mod(y + step, NY)) for step in (1, NY - 1)]
 
     barrier = pltpu.get_barrier_semaphore()
-    pl.semaphore_signal(barrier, inc=1, device_id=sib, device_id_type=MESH)
+    for to in [sib] + beside:
+        pl.semaphore_signal(barrier, inc=1, device_id=to, device_id_type=MESH)
     for j in range(1, NX):
-        pl.semaphore_signal(barrier, inc=1, device_id=device((x + j) % NX, y, z, c), device_id_type=MESH)
-    for step in (1, NY - 1):
-        pl.semaphore_signal(barrier, inc=1, device_id=device(x, (y + step) % NY, z, c), device_id_type=MESH)
+        pl.semaphore_signal(barrier, inc=1, device_id=here.at_x(mod(x + j, NX)), device_id_type=MESH)
     for j in range(1, NZ):
-        pl.semaphore_signal(barrier, inc=1, device_id=device(x, y, (z + j) % NZ, c), device_id_type=MESH)
+        pl.semaphore_signal(barrier, inc=1, device_id=here.at_z(mod(z + j, NZ)), device_id_type=MESH)
 
     mine_here = pltpu.make_async_copy(inv.at[pl.ds(pl.multiple_of(32 * x, 32), 32)], kept.at[q, z, x], s_l)
     mine_here.start()
+    pl.semaphore_wait(barrier, 1 + (NX - 1) + 2 + (NZ - 1))
+    for j in (2, 1, 3):
+        to = mod(x + j, NX)
+        send(inv.at[pl.ds(pl.multiple_of(32 * to, 32), 32)], kept.at[q, z, x],
+             s_p.at[j - 1], r_p.at[j - 1], here.at_x(to))
+    mine_here.wait()
+    for j in range(1, NX):
+        arrived(kept.at[q, z, mod(x - j + NX, NX)], r_p.at[j - 1])
+    for j in FAR_FIRST:
+        send(kept.at[q, z], kept.at[q, z], s_z.at[j - 1], r_z.at[j - 1], here.at_z(mod(z + j, NZ)))
+
+    def to_neighbours(zz, j):
+        for k in range(2):
+            half = kept.at[q, zz, pl.ds(2 * k, 2)]
+            send(half, half, s_q.at[j, k], r_q.at[j, k], beside[k])
+
+    to_neighbours(z, 0)
 
     def find_a(b, found):
         at = owner_a[b] - 3 * own
@@ -371,43 +407,25 @@
     slot_g = lax.fori_loop(0, 32, find_g, zero)
 
     def at_a(b):
-        return b % 2, (b % 48) // 6, (b % 6) // 2
+        return mod(b, 2), lax.div(mod(b, 48), 6), lax.div(mod(b, 6), 2)
 
     def at_g(b):
-        return b % 2, (b % 16) // 2, 3
+        return mod(b, 2), lax.div(mod(b, 16), 2), 3
 
     def entry(core, k):
         if k == 3:
-            return slot_g // 16, at_g(slot_g)
+            return lax.div(slot_g, 16), at_g(slot_g)
         block = jnp.where(core == 0, slot_a[k], 3 * own + k)
-        return block // 48, at_a(block)
+        return lax.div(block, 48), at_a(block)
 
     mine = [entry(c, k) for k in range(4)]
     theirs = [entry(1 - c, k) for k in range(4)]
-    mine_here.wait()
-    pl.semaphore_wait(barrier, 1 + (NX - 1) + 2 + (NZ - 1))
-
-    for j in range(1, NX):
-        to = (x + j) % NX
-        send(inv.at[pl.ds(pl.multiple_of(32 * to, 32), 32)], kept.at[q, z, x],
-             s_p.at[j - 1], r_p.at[j - 1], device(to, y, z, c))
-    for j in range(1, NX):
-        arrived(kept.at[q, z, (x - j + NX) % NX], r_p.at[j - 1])
-    for j in range(1, NZ):
-        send(kept.at[q, z], kept.at[q, z], s_z.at[j - 1], r_z.at[j - 1], device(x, y, (z + j) % NZ, c))
-
-    def to_neighbours(zz, j):
-        for k, step in enumerate((1, NY - 1)):
-            half = kept.at[q, zz, pl.ds(2 * k, 2)]
-            send(half, half, s_q.at[j, k], r_q.at[j, k], device(x, (y + step) % NY, z, c))
-
-    to_neighbours(z, 0)
-    for j in range(1, NZ):
-        zz = (z - j + NZ) % NZ
+    for j in FAR_FIRST:
+        zz = mod(z - j + NZ, NZ)
         arrived(kept.at[q, zz], r_z.at[j - 1])
         to_neighbours(zz, j)
     for j in range(NZ):
-        zz = (z - j + NZ) % NZ
+        zz = mod(z - j + NZ, NZ)
         for k in range(2):
             arrived(kept.at[1 - q, zz, pl.ds(2 * k, 2)], r_q.at[j, k])
 
@@ -421,22 +439,22 @@
     arrived(er, r_e.at[0])
     values = [jnp.where(mine[k][0] == c, values[k], er[k]) for k in range(4)]
     for j in range(1, NX + 1):
-        to = (x + j) % NX
+        to = mod(x + j, NX)
         for k in range(4):
             s4[to, k] = values[k]
         for k in range(2):
-            here = kept[at_g(8 * to + 4 * yh + 2 * c + k)]
-            s4[to, 4 + k] = jnp.where(to // 2 == c, here, er[4 + 2 * (to % 2) + k])
+            own_half = kept[at_g(8 * to + 4 * yh + 2 * c + k)]
+            s4[to, 4 + k] = jnp.where(lax.div(to, 2) == c, own_half, er[4 + 2 * mod(to, 2) + k])
         if j < NX:
-            send(s4.at[to], r4.at[x], s_4.at[j - 1], r_4.at[j - 1], device(to, y, z, c))
+            send(s4.at[to], r4.at[x], s_4.at[j - 1], r_4.at[j - 1], here.at_x(to))
     r4[x] = s4[x]
     send(s4.at[x, pl.ds(0, 4)], r5.at[x], s_5.at[0], r_5.at[0], sib)
     for j in range(1, NX):
-        frm = (x - j + NX) % NX
+        frm = mod(x - j + NX, NX)
         arrived(r4.at[frm], r_4.at[j - 1])
         send(r4.at[frm, pl.ds(0, 4)], r5.at[frm], s_5.at[j], r_5.at[j], sib)
     for j in range(NX):
-        arrived(r5.at[(x - j + NX) % NX], r_5.at[j])
+        arrived(r5.at[mod(x - j + NX, NX)], r_5.at[j])
 
     for j in range(NZ):
         for k in range(2):
@@ -472,7 +490,7 @@
 
 
 def apply_kernel(r4_hbm, r5_hbm, w_hbm, a_hbm, g_hbm, p_hbm, r4, r5, w, a_out, g_out, p_out, s_in, s_out):
-    _, _, _, c = place()
+    c = Place().c
     loads = [
         pltpu.make_async_copy(src, dst, s_in.at[k])
         for k, (src, dst) in enumerate(((r4_hbm, r4), (r5_hbm, r5), (w_hbm, w)))
@@ -533,8 +551,7 @@
     token_total = hidden_act.shape[0] * lax.axis_size("own") * lax.axis_size("dp")
     packed, extra = gram_sums(hidden_act, out_grad)
     inverse = newton(token_total, packed, extra)
-    r4, r5 = spread(inverse, owner_a, owner_g)
-    return apply_inverses(r4, r5, weight_grad)
+    return apply_inverses(*spread(inverse, owner_a, owner_g), weight_grad)
 
 
 def solution(mesh):

time: 85.4 us -> 85.8 us (level)
    pallas_call x1, Pallas kernels: 50.5 us -> 52 us  [gram_sums(): pl.pallas_call(gram_kernel, out_shape=(jax.ShapeDtypeStruct((NY, 2) + til...]
where the time goes in v6:
time: 85.8 us; the launch traced here: 85.5 us
  Pallas kernels  84.9 us (99%)
    pallas_call x1, Pallas kernels, gram_sums(): pl.pallas_call(gram_kernel, out_shape=(jax.ShapeDtypeStruct((NY, 2) + til...  52 us
    pallas_call x1, Pallas kernels, spread(): pl.pallas_call(spread_kernel, out_shape=(jax.ShapeDtypeStruct((NX, 6) + p...  26.3 us
    pallas_call x1, Pallas kernels, newton(): pl.pallas_call(lambda *refs: newton_kernel(token_total, *refs), out_shape...  4.39 us
    pallas_call x1, Pallas kernels, apply_inverses(): pl.pallas_call(apply_kernel, out_shape=outs, in_specs=[pl.BlockSpec(memor...  2.23 us

profile of v6, /device:TPU:1, one launch (start us, length us, event | category | flops | bytes accessed | tf_op | source)
XLA Modules:
  0.0 85.5 jit_solution(13139615591496331334)
XLA Ops:
  0.6 52.0 %gram_sums.1 = (f32[8,2,8,128]{3,2,1,0:T(8,128)}, f32[8,128]{1,0:T(8,128)}) custom-call(bf16[128,12288]{1,0:T(8,128)(2,1)} %hid.1, bf16[128,4096]{1,0:T(8,128)(2,1)} %grd.1), custom_call_target="tpu_custom_call" | custom-call | flops 536870912 | bytes 4194304 | tf_op jit(solution)/shard_map/gram_sums/pallas_call | solution.py:253
  52.6 4.4 %newton.1.inv = bf16[128,128]{1,0:T(8,128)(2,1)} custom-call(f32[8,2,8,128]{3,2,1,0:T(8,128)} %get-tuple-element.7.refs_0_, f32[8,128]{1,0:T(8,128)} %get-tuple-element.8.refs_1_), custom_call_target="tpu_custom_call" | custom-call | tf_op jit(solution)/shard_map/newton/pallas_call | solution.py:351
  57.0 26.3 %spread_inverses.1 = (bf16[4,6,32,128]{3,2,1,0:T(8,128)(2,1)}, bf16[4,4,32,128]{3,2,1,0:T(8,128)(2,1)}) custom-call(bf16[128,128]{1,0:T(8,128)(2,1)} %newton.1.inv, s32[96]{0:T(128)} %owner_a.1, s32[32]{0:T(128)} %owner_g.1), custom_call_target="tpu_custom_call" | custom-call | tf_op jit(solution)/shard_map/spread_inverses/pallas_call | solution.py:477
  83.3 2.2 %apply_inverses.1 = (bf16[3,128,128]{2,1,0:T(8,128)(2,1)}, bf16[1,128,128]{2,1,0:T(8,128)(2,1)}, f32[384,256]{1,0:T(8,128)}) custom-call(bf16[4,6,32,128]{3,2,1,0:T(8,128)(2,1)} %get-tuple-element.9.r4_hbm, bf16[4,4,32,128]{3,2,1,0:T(8,128)(2,1)} %get-tuple-element.10.r5_hbm, bf16[384,256]{1,0:T(8,128)(2,1)} %w_hbm.1), custom_call_target="tpu_custom_call" | custom-call | tf_op jit(solution)/shard_map/apply_inverses/pallas_call | solution.py:538
